TPU v7x, 256 devices: a whole 4x4x8 slice. The times are simulated.
256 devices in a mesh: gx: 16 (over x, y), gy: 16 (over z, core).
Axes of the slice: x: 4, y: 4, z: 8, core: 2. Of those that a mesh axis runs over, the one named last changes fastest.
Arguments:
- source: float32 [8, 8, 32, 64, 256], P(None, None, 'gx', 'gy'), may hold values from -6 to 6
- geometry: float32 [3, 32, 64, 32], P(None, 'gx', 'gy'), may hold values from 0.5 to 2
- disc_mask: int32 [32, 64, 32], P('gx', 'gy'), may hold values 0 or 1
- thrust: float32 [32, 64, 32], P('gx', 'gy'), may hold values from 0.5 to 4
- xxt_factor: float32 [9, 32, 524288], P(None, None, ('gx', 'gy')), as said below
- col_count: int32 [9, 256], P(None, ('gx', 'gy')), may hold values from 8 to 32, as said below
Outputs:
- pressure: float32 [8, 8, 32, 64, 256], P(None, None, 'gx', 'gy')
Inputs may be any that keep to these rules, and one draw needn't show every extreme that they name: `col_count`: equal on all devices of a level-l group (flat device index along gx+gy agreeing after the lowest l bits are dropped); at every level some group has exactly 32. `xxt_factor`: Real-valued entries of order one or below.
All inputs are finite; a program needn't handle non-finite values. No bound on the sum of `disc_mask` on one device may be relied on, other than what follows from the above.
Results may differ from a plain program's by a relative error of at most 0.00018.
Values sent between devices are 32-bit elements; how exact they have to be, the bound alone decides.
A program may use at most 128 MiB of HBM per device.

v0:
```python
import functools
import math

import jax
import jax.numpy as jnp
import ml_dtypes
import numpy as np
from jax import lax
from jax.experimental import pallas as pl
from jax.experimental.pallas import tpu as pltpu
from jax.sharding import PartitionSpec as P

NODES = 8
CYCLES = 2
EX = 2
EY = 4
EZ = 32
LANES = EY * EZ
XCOLS = 32
SMOOTH = 5

bound_low = 0.3
bound_high = 3.0
shift_ratio = 0.25
MESH = pl.DeviceIdType.MESH


def legendre_table(points, poly_order):
    table = [points * 0.0 + 1.0, points]
    for degree in range(2, poly_order + 1):
        table.append(
            ((2.0 * degree - 1.0) * points * table[-1] - (degree - 1.0) * table[-2]) / degree
        )
    return table


def jacobi_eigen(matrix):
    size_n = matrix.shape[0]
    current = matrix.copy()
    vectors = np.eye(size_n)
    for sweep_index in range(30):
        for first in range(size_n - 1):
            for second in range(first + 1, size_n):
                angle = 0.5 * math.atan2(
                    2.0 * float(current[first, second]),
                    float(current[second, second] - current[first, first]),
                )
                rotation = np.eye(size_n)
                rotation[first, first] = math.cos(angle)
                rotation[second, second] = math.cos(angle)
                rotation[first, second] = math.sin(angle)
                rotation[second, first] = -math.sin(angle)
                current = rotation.T @ current @ rotation
                vectors = vectors @ rotation
    values = np.array([current[index, index] for index in range(size_n)])
    order = np.argsort(values)
    return (values[order], vectors[:, order])


def gll_tables(node_count):
    poly_order = node_count - 1
    points = np.cos(np.pi * np.arange(node_count) / poly_order)
    for newton_index in range(200):
        table = legendre_table(points, poly_order)
        points = points - (points * table[poly_order] - table[poly_order - 1]) / (
            node_count * table[poly_order]
        )
    points = points[::-1].copy()
    legendre = legendre_table(points, poly_order)[poly_order]
    weights = 2.0 / (poly_order * (poly_order + 1) * legendre**2)
    identity = np.eye(node_count)
    gap_matrix = points[:, None] - points[None, :] + identity
    off_diagonal = legendre[:, None] / (legendre[None, :] * gap_matrix) * (1.0 - identity)
    end_value = poly_order * (poly_order + 1) / 4.0
    end_terms = np.concatenate([[-end_value], np.zeros(node_count - 2), [end_value]])
    derivative = off_diagonal + identity * end_terms[None, :]
    stiffness = derivative.T @ (weights[:, None] * derivative)
    root_inverse = 1.0 / np.sqrt(weights)
    symmetric = root_inverse[:, None] * stiffness * root_inverse[None, :]
    symmetric = 0.5 * (symmetric + symmetric.T)
    eigen_values, eigen_vectors = jacobi_eigen(symmetric)
    eigen_modes = root_inverse[:, None] * eigen_vectors
    vertex_interp = np.stack([(1.0 - points) / 2.0, (1.0 + points) / 2.0], axis=1)
    return weights, eigen_modes, eigen_values, vertex_interp


def mode_order(modes):
    even = [i for i in range(NODES) if modes[0, i] * modes[NODES - 1, i] > 0.0]
    odd = [i for i in range(NODES) if i not in even]
    return even, odd


def split_pair(matrix):
    exact = matrix.astype(np.float32)
    high = exact.astype(ml_dtypes.bfloat16)
    low = (exact - high.astype(np.float32)).astype(ml_dtypes.bfloat16)
    return np.concatenate([high, high, low], axis=1)


def constant_tables():
    weights, modes, values, interp = gll_tables(NODES)
    even, odd = mode_order(modes)
    half = NODES // 2
    mats = []
    for chosen in (even, odd):
        inverse = np.kron(modes[:half][:, chosen], np.kron(modes, modes))
        mats.append((split_pair(inverse.T), split_pair(inverse)))
    matrices = np.stack([mats[0][0], mats[1][0], mats[0][1], mats[1][1]])
    full = np.ones((NODES, LANES))
    edge = np.ones(NODES)
    edge[0] = edge[-1] = 0.5
    ez = np.arange(LANES)[None, :] % EZ
    node = np.arange(NODES)[:, None]
    z_shared = 1.0 + ((node == 0) & (ez > 0)) + ((node == NODES - 1) & (ez < EZ - 1))
    free = 1.0 - ((node == NODES - 1) & (ez == EZ - 1))
    rows = [values[i] * full for i in even + odd]
    rows += [value * full for value in values]
    rows += [weight * full for weight in weights]
    rows += [value * full for value in edge]
    rows += [values[:, None] * full, weights[:, None] * full, free / z_shared, free * full]
    rows += [interp[:, 0:1] * full, interp[:, 1:2] * full]
    table = np.stack(rows).astype(np.float32)
    perm = np.zeros((2 * LANES, 2 * LANES), np.float32)
    for t in range(2):
        for element in range(LANES):
            perm[t * LANES + element, 2 * element + t] = 1.0
    perms = np.stack([perm, perm.T]).astype(ml_dtypes.bfloat16)
    return matrices, table, perms, interp.astype(np.float32)


def flipped(index, bits):
    out = index
    bit = 1
    while bit <= bits:
        if bits & bit:
            out = out + bit - 2 * bit * lax.rem(lax.div(index, bit), 2)
        bit *= 2
    return out


def exact_rows(value, perm):
    first = value.astype(jnp.bfloat16)
    rest = value - first.astype(jnp.float32)
    second = rest.astype(jnp.bfloat16)
    third = (rest - second.astype(jnp.float32)).astype(jnp.bfloat16)
    parts = [
        jnp.dot(part, perm, preferred_element_type=jnp.float32)
        for part in (first, second, third)
    ]
    return parts[0] + parts[1] + parts[2]


def kernel(
    n_gx,
    n_gy,
    levels,
    interp,
    source_ref,
    geom_ref,
    force_ref,
    live_ref,
    x_factor_ref,
    mat_ref,
    tab_ref,
    perm_ref,
    out_ref,
    u_ref,
    r_ref,
    d_ref,
    weight_ref,
    winv_ref,
    lam_ref,
    inv_ref,
    send_x,
    send_y,
    send_c,
    recv_x,
    recv_y,
    recv_c,
    send_one,
    recv_one,
    send_two,
    recv_two,
    send_sem,
    recv_sem,
    one_send_sem,
    one_recv_sem,
    two_send_sem,
    two_recv_sem,
):
    me_x = lax.axis_index("gx")
    me_y = lax.axis_index("gy")
    left = lax.rem(me_x + n_gx - 1, n_gx)
    right = lax.rem(me_x + 1, n_gx)
    down = lax.rem(me_y + n_gy - 1, n_gy)
    up = lax.rem(me_y + 1, n_gy)
    targets = [
        (left, me_y),
        (right, me_y),
        (me_x, down),
        (me_x, up),
        (left, down),
        (right, up),
        (left, up),
        (right, down),
    ]
    one_targets = [(me_x, flipped(me_y, off)) for off in range(1, n_gy)]
    two_targets = [(flipped(me_x, off), me_y) for off in range(1, n_gx)]
    barrier = pltpu.get_barrier_semaphore()
    everyone = targets + one_targets + two_targets
    for target in everyone:
        pl.semaphore_signal(barrier, inc=1, device_id=target, device_id_type=MESH)

    lane = lax.broadcasted_iota(jnp.int32, (1, 1, 1, LANES), 3)
    lane3 = lax.broadcasted_iota(jnp.int32, (1, 1, LANES), 2)
    lane2 = lax.broadcasted_iota(jnp.int32, (1, LANES), 1)
    ez = lax.rem(lane, EZ)

    def roll(value, shift):
        shift = shift % LANES
        return value if shift == 0 else pltpu.roll(value, shift, value.ndim - 1)

    lam_i = tab_ref[0:8]
    lam_j = tab_ref[8:16]
    w_node = tab_ref[16:24]
    edge = tab_ref[24:32]
    lam_k = tab_ref[32]
    w_c = tab_ref[33]
    zmask = tab_ref[34]
    free = tab_ref[35]
    weight_ref[...] = (w_node[:, None] * w_node[None] * w_c[None, None]).reshape(8, 64, LANES)
    winv_ref[...] = (edge[:, None] * edge[None] * zmask[None, None]).reshape(8, 64, LANES)
    for ex in range(EX):
        hx = geom_ref[0, ex : ex + 1]
        hy = geom_ref[1, ex : ex + 1]
        hz = geom_ref[2, ex : ex + 1]
        ax = hy * hz / (2.0 * hx)
        ay = hx * hz / (2.0 * hy)
        az = hx * hy / (2.0 * hz)
        in_x = lam_i * ax[None]
        in_y = lam_j * ay[None]
        in_z = lam_k * az
        spectrum = (in_x[:, None] + in_y[None] + in_z[None, None]).reshape(8, 64, LANES)
        shift = shift_ratio * (ax + ay + az)
        lam_ref[ex] = spectrum
        inv_ref[ex] = 1.0 / (spectrum + shift[None])
        mass = (hx * hy * hz / 8.0)[None] * weight_ref[...]
        u_ref[ex] = mass * (source_ref[ex] + force_ref[ex : ex + 1][None])

    def free_scaled(value):
        return (value.reshape(8, 8, 8, LANES) * free[None, None]).reshape(8, 64, LANES)

    for ex in range(EX):
        u_ref[ex] = free_scaled(u_ref[ex])

    pl.semaphore_wait(barrier, len(everyone))

    def assemble(slot):
        shared = u_ref[0, 7] + u_ref[1, 0]
        u_ref[0, 7] = shared
        u_ref[1, 0] = shared
        low = u_ref[:, :, 0:8]
        high = u_ref[:, :, 56:64]
        u_ref[:, :, 0:8] = low + jnp.where(lane >= EZ, roll(high, EZ), 0.0)
        u_ref[:, :, 56:64] = high + jnp.where(lane < LANES - EZ, roll(low, -EZ), 0.0)
        for ex in range(EX):
            for a in range(NODES):
                low = u_ref[ex, a, pl.ds(0, 8, stride=8)]
                high = u_ref[ex, a, pl.ds(7, 8, stride=8)]
                z2 = lax.rem(lane2, EZ)
                u_ref[ex, a, pl.ds(0, 8, stride=8)] = low + jnp.where(
                    z2 > 0, roll(high, 1), 0.0
                )
                u_ref[ex, a, pl.ds(7, 8, stride=8)] = high + jnp.where(
                    z2 < EZ - 1, roll(low, -1), 0.0
                )
        send_x[slot, 0] = u_ref[0, 0]
        send_x[slot, 1] = u_ref[1, 7]
        send_c[slot, 0] = u_ref[0, 0, 0:8]
        send_c[slot, 1] = u_ref[1, 7, 56:64]
        send_c[slot, 2] = u_ref[0, 0, 56:64]
        send_c[slot, 3] = u_ref[1, 7, 0:8]
        for ex in range(EX):
            for which, first, ey in ((0, 0, 0), (1, 56, EY - 1)):
                packed = None
                for s in range(4):
                    face = roll(
                        u_ref[ex, 2 * s : 2 * s + 2, first : first + 8], EZ * (s - ey)
                    )
                    packed = (
                        face if packed is None else jnp.where(lane3 >= EZ * s, face, packed)
                    )
                send_y[slot, which, ex] = packed
        pairs = (
            [(send_x.at[slot, i], recv_x.at[slot, i]) for i in range(2)]
            + [(send_y.at[slot, i], recv_y.at[slot, i]) for i in range(2)]
            + [(send_c.at[slot, i], recv_c.at[slot, i]) for i in range(4)]
        )
        copies = []
        for index, (source, landing) in enumerate(pairs):
            copy = pltpu.make_async_remote_copy(
                src_ref=source,
                dst_ref=landing,
                send_sem=send_sem.at[slot, index],
                recv_sem=recv_sem.at[slot, index],
                device_id=targets[index],
                device_id_type=MESH,
            )
            copy.start()
            copies.append(copy)
        for copy in copies:
            copy.wait()
        u_ref[1, 7] += recv_x[slot, 0]
        u_ref[0, 0] += recv_x[slot, 1]
        for ex in range(EX):
            for which, first, ey in ((0, 56, EY - 1), (1, 0, 0)):
                packed = recv_y[slot, which, ex]
                inside = (lane3 >= EZ * ey) & (lane3 < EZ * (ey + 1))
                for s in range(4):
                    u_ref[ex, 2 * s : 2 * s + 2, first : first + 8] += jnp.where(
                        inside, roll(packed, EZ * (ey - s)), 0.0
                    )
        for index, (ex, a, first, to_ey, from_ey) in enumerate(
            (
                (1, 7, 56, EY - 1, 0),
                (0, 0, 0, 0, EY - 1),
                (1, 7, 0, 0, EY - 1),
                (0, 0, 56, EY - 1, 0),
            )
        ):
            inside = (lane2 >= EZ * to_ey) & (lane2 < EZ * (to_ey + 1))
            u_ref[ex, a, first : first + 8] += jnp.where(
                inside, roll(recv_c[slot, index], EZ * (to_ey - from_ey)), 0.0
            )

    def product(which, value):
        high = value.astype(jnp.bfloat16)
        low = (value - high.astype(jnp.float32)).astype(jnp.bfloat16)
        return jnp.dot(
            mat_ref[which],
            jnp.concatenate([high, low, high], axis=0),
            preferred_element_type=jnp.float32,
        )

    def flat(parts):
        return jnp.concatenate([part.reshape(256, LANES) for part in parts], axis=1)

    def element_op(fields, diag_ref):
        even, odd = [], []
        for field in fields:
            low = field[0:4]
            high = jnp.concatenate([field[7:8], field[6:7], field[5:6], field[4:5]], axis=0)
            even.append(low + high)
            odd.append(low - high)
        even = product(0, flat(even)) * flat([diag_ref[ex, 0:4] for ex in range(EX)])
        odd = product(1, flat(odd)) * flat([diag_ref[ex, 4:8] for ex in range(EX)])
        even = product(2, even)
        odd = product(3, odd)
        out = []
        for ex in range(EX):
            at = slice(ex * LANES, (ex + 1) * LANES)
            e = even[:, at].reshape(4, 64, LANES)
            o = odd[:, at].reshape(4, 64, LANES)
            diff = e - o
            out.append(
                jnp.concatenate([e + o, diff[3:4], diff[2:3], diff[1:2], diff[0:1]], axis=0)
            )
        return out

    def stiffness():
        weight = weight_ref[...]
        out = element_op([d_ref[ex] * weight for ex in range(EX)], lam_ref)
        for ex in range(EX):
            u_ref[ex] = free_scaled(out[ex] * weight)

    def smoother():
        out = element_op([r_ref[ex] for ex in range(EX)], inv_ref)
        for ex in range(EX):
            u_ref[ex] = out[ex] * winv_ref[...]

    wide = (levels - 1) * XCOLS
    gy_bits = n_gy.bit_length() - 1
    split = gy_bits * XCOLS

    def exchange(cycle, send_ref, recv_ref, to, send_s, recv_s):
        copies = []
        for index, target in enumerate(to):
            copy = pltpu.make_async_remote_copy(
                src_ref=send_ref,
                dst_ref=recv_ref.at[cycle, index],
                send_sem=send_s.at[index],
                recv_sem=recv_s.at[cycle, index],
                device_id=target,
                device_id_type=MESH,
            )
            copy.start()
            copies.append(copy)
        for copy in copies:
            copy.wait()

    def level_sum(own, recv_ref, cycle, count, first_level_lane):
        which = lax.broadcasted_iota(jnp.int32, own.shape, 1)
        total = own
        start = 1
        bit = 0
        while start < count:
            part = recv_ref[cycle, start - 1]
            for index in range(start + 1, 2 * start):
                part = part + recv_ref[cycle, index - 1]
            total = total + jnp.where(which >= bit * XCOLS + first_level_lane, part, 0.0)
            start *= 2
            bit += 1
        return total

    def coarse(cycle):
        columns = []
        for t in range(2):
            to_t = tab_ref[36 + t]
            rows = []
            for v in range(2):
                for u in range(2):
                    for ex in range(EX):
                        rows.append((v, u, ex))
            columns.append(rows)
        sums = {}
        for ex in range(EX):
            scaled = r_ref[ex] * winv_ref[...]
            for v in range(2):
                by_v = scaled[0] * float(interp[0, v])
                for a in range(1, NODES):
                    by_v = by_v + scaled[a] * float(interp[a, v])
                by_v = by_v.reshape(8, 8, LANES)
                for u in range(2):
                    by_u = by_v[0] * float(interp[0, u])
                    for b in range(1, NODES):
                        by_u = by_u + by_v[b] * float(interp[b, u])
                    for t in range(2):
                        sums[v, u, ex, t] = jnp.sum(
                            by_u * tab_ref[36 + t], axis=0, keepdims=True
                        )
        order = [(v, u, ex) for v in range(2) for u in range(2) for ex in range(EX)]
        split_t = jnp.concatenate(
            [jnp.concatenate([sums[key + (t,)] for t in range(2)], axis=1) for key in order],
            axis=0,
        )
        vector = exact_rows(split_t, perm_ref[0])
        pieces = []
        for level in range(levels):
            rows = slice(level * XCOLS, (level + 1) * XCOLS)
            acc = None
            for q in range(8):
                term = x_factor_ref[rows, q * 256 : (q + 1) * 256] * vector[q : q + 1]
                acc = term if acc is None else acc + term
            pieces.append(acc[:, :LANES] + acc[:, LANES:])
        def row_of(parts):
            block = jnp.concatenate(parts, axis=0)
            missing = LANES - block.shape[0]
            if missing:
                block = jnp.concatenate([block, jnp.zeros((missing, LANES), jnp.float32)], axis=0)
            return jnp.sum(block.T, axis=0, keepdims=True)
        own = row_of(pieces[0:1])
        upper = jnp.concatenate(
            [row_of(pieces[i : i + 4]) for i in range(1, levels, 4)], axis=1
        )[:, :wide]
        send_one[...] = upper
        exchange(cycle, send_one, recv_one, one_targets, one_send_sem, one_recv_sem)
        upper = level_sum(upper, recv_one, cycle, n_gy, 0)
        send_two[...] = upper[:, split:]
        exchange(cycle, send_two, recv_two, two_targets, two_send_sem, two_recv_sem)
        top = level_sum(upper[:, split:], recv_two, cycle, n_gx, 0)
        upper = jnp.concatenate([upper[:, :split], top], axis=1)
        own = own * live_ref[:, 0:LANES]
        upper = upper * live_ref[:, LANES : LANES + wide]
        tail = (-wide) % LANES
        if tail:
            upper = jnp.concatenate([upper, jnp.zeros((1, tail), jnp.float32)], axis=1)
        cols = [jnp.broadcast_to(own, (LANES, LANES)).T[:XCOLS]]
        for first in range(0, wide, LANES):
            part = jnp.broadcast_to(upper[:, first : first + LANES], (LANES, LANES)).T
            cols += [part[k * XCOLS : (k + 1) * XCOLS] for k in range(LANES // XCOLS)]
        back = []
        for q in range(8):
            acc = None
            for level in range(levels):
                block = x_factor_ref[
                    level * XCOLS : (level + 1) * XCOLS, q * 256 : (q + 1) * 256
                ]
                col = cols[level]
                term = block * jnp.concatenate([col, col], axis=1)
                acc = term if acc is None else acc + term
            back.append(jnp.sum(acc, axis=0, keepdims=True))
        split_t = exact_rows(jnp.concatenate(back, axis=0), perm_ref[1])
        for ex in range(EX):
            by_v = []
            for v in range(2):
                by_u = []
                for u in range(2):
                    q = (v * 2 + u) * EX + ex
                    by_u.append(
                        split_t[q : q + 1, :LANES] * tab_ref[36]
                        + split_t[q : q + 1, LANES:] * tab_ref[37]
                    )
                by_v.append(
                    jnp.concatenate(
                        [
                            by_u[0] * float(interp[b, 0]) + by_u[1] * float(interp[b, 1])
                            for b in range(NODES)
                        ],
                        axis=0,
                    )
                )
            for a in range(NODES):
                u_ref[ex, a] = winv_ref[a] * (
                    by_v[0] * float(interp[a, 0]) + by_v[1] * float(interp[a, 1])
                )

    center = 0.5 * (bound_high + bound_low)
    radius = 0.5 * (bound_high - bound_low)
    ratio = center / radius
    rho_old = 1.0 / ratio
    rho_new = 1.0 / (2.0 * ratio - rho_old)

    assemble(1)
    r_ref[...] = u_ref[...]
    d_ref[...] = jnp.zeros_like(d_ref)
    out_ref[...] = jnp.zeros_like(out_ref)

    def step(index, carry):
        phase = lax.rem(index, SMOOTH)
        cycle = lax.div(index, SMOOTH)
        is_coarse = phase == 2
        second = (phase == 1) | (phase == 4)
        keep = jnp.where(second, rho_new * rho_old, 0.0)
        take = jnp.where(second, 2.0 * rho_new / radius, 1.0 / center)
        take = jnp.where(is_coarse, 1.0, take)

        @pl.when(is_coarse)
        def _():
            coarse(cycle)

        @pl.when(jnp.logical_not(is_coarse))
        def _():
            smoother()

        assemble(0)
        for ex in range(EX):
            direction = keep * d_ref[ex] + take * u_ref[ex]
            d_ref[ex] = direction
            out_ref[ex] += direction

        @pl.when(index < SMOOTH * CYCLES - 1)
        def _():
            stiffness()
            assemble(1)
            for ex in range(EX):
                r_ref[ex] -= u_ref[ex]

        return carry

    lax.fori_loop(0, SMOOTH * CYCLES, step, 0)


def per_device(source, geometry, disc_mask, thrust, xxt_factor, col_count):
    n_gx = lax.axis_size("gx")
    n_gy = lax.axis_size("gy")
    levels = xxt_factor.shape[0]
    wide = (levels - 1) * XCOLS
    split = (n_gy.bit_length() - 1) * XCOLS
    matrices, table, perms, interp = constant_tables()
    nodes = source.reshape(NODES, NODES, EX, EY, EZ, NODES)
    nodes = nodes.transpose(2, 0, 1, 5, 3, 4).reshape(EX, NODES, 64, LANES)
    geom = geometry.reshape(3, EX, LANES)
    force = (disc_mask.astype(jnp.float32) * thrust).reshape(EX, LANES)
    live = (jnp.arange(XCOLS)[None, :] < col_count).astype(jnp.float32)
    live = jnp.concatenate(
        [
            live[0:1],
            jnp.zeros((1, LANES - XCOLS), jnp.float32),
            live[1:].reshape(1, wide),
        ],
        axis=1,
    )
    field = (EX, NODES, 64, LANES)
    f32 = jnp.float32
    out = pl.pallas_call(
        functools.partial(kernel, n_gx, n_gy, levels, interp),
        out_shape=jax.ShapeDtypeStruct(field, f32),
        in_specs=[pl.BlockSpec(memory_space=pltpu.VMEM)] * 8,
        out_specs=pl.BlockSpec(memory_space=pltpu.VMEM),
        scratch_shapes=[
            pltpu.VMEM(field, f32),
            pltpu.VMEM(field, f32),
            pltpu.VMEM(field, f32),
            pltpu.VMEM(field[1:], f32),
            pltpu.VMEM(field[1:], f32),
            pltpu.VMEM(field, f32),
            pltpu.VMEM(field, f32),
            pltpu.VMEM((2, 2, 64, LANES), f32),
            pltpu.VMEM((2, 2, EX, 2, 8, LANES), f32),
            pltpu.VMEM((2, 4, 8, LANES), f32),
            pltpu.VMEM((2, 2, 64, LANES), f32),
            pltpu.VMEM((2, 2, EX, 2, 8, LANES), f32),
            pltpu.VMEM((2, 4, 8, LANES), f32),
            pltpu.VMEM((1, wide), f32),
            pltpu.VMEM((CYCLES, n_gy - 1, 1, wide), f32),
            pltpu.VMEM((1, wide - split), f32),
            pltpu.VMEM((CYCLES, n_gx - 1, 1, wide - split), f32),
            pltpu.SemaphoreType.DMA((2, 8)),
            pltpu.SemaphoreType.DMA((2, 8)),
            pltpu.SemaphoreType.DMA((n_gy - 1,)),
            pltpu.SemaphoreType.DMA((CYCLES, n_gy - 1)),
            pltpu.SemaphoreType.DMA((n_gx - 1,)),
            pltpu.SemaphoreType.DMA((CYCLES, n_gx - 1)),
        ],
        compiler_params=pltpu.CompilerParams(
            collective_id=0, has_side_effects=True, vmem_limit_bytes=48 * 1024 * 1024
        ),
    )(
        nodes,
        geom,
        force,
        live,
        xxt_factor.reshape(levels * XCOLS, xxt_factor.shape[2]),
        jnp.asarray(matrices),
        jnp.asarray(table),
        jnp.asarray(perms),
    )
    out = out.reshape(EX, NODES, NODES, NODES, EY, EZ).transpose(1, 2, 0, 4, 5, 3)
    return out.reshape(source.shape)


def solution(mesh):
    return jax.shard_map(
        per_device,
        mesh=mesh,
        in_specs=(
            P(None, None, "gx", "gy", None),
            P(None, "gx", "gy", None),
            P("gx", "gy", None),
            P("gx", "gy", None),
            P(None, None, ("gx", "gy")),
            P(None, ("gx", "gy")),
        ),
        out_specs=P(None, None, "gx", "gy", None),
        check_vma=False,
    )
```

profile of v0, /device:TPU:1, one launch (start us, length us, event | category | flops | bytes accessed | tf_op | source)
XLA Modules:
  0.0 188.4 jit_solution(13464886092052026822)
XLA Ops:
  0.0 1.2 copy.12
  1.2 6.2 %reshape.24 = f32[8,8,2,4,32,8]{5,4,1,3,2,0:T(8,128)} reshape(f32[8,8,2,4,256]{4,1,3,2,0:T(8,128)S(1)} %copy.12) | data formatting | bytes 1048576 | tf_op jit(solution)/shard_map/reshape | solution.py:570
  7.4 6.3 %copy.13 = f32[2,8,8,8,4,32]{5,4,3,2,1,0:T(4,128)} copy(f32[2,8,8,8,4,32]{3,5,2,4,0,1:T(8,128)} %bitcast.18) | data formatting | bytes 1048576 | tf_op jit(solution)/shard_map/transpose | solution.py:571
  13.7 0.0 copy-start
  13.7 2.6 %reshape.25.source_ref = f32[2,8,64,128]{3,2,1,0:T(8,128)S(1)} reshape(f32[2,8,8,8,4,32]{5,4,3,2,1,0:T(4,128)} %copy.13) | data formatting | bytes 1048576 | tf_op jit(solution)/shard_map/reshape | solution.py:571
  16.3 0.0 copy-done.4
  16.3 0.1 reshape.26.geom_ref
  16.4 0.0 copy-done.5
  16.4 0.0 copy-done.6
  16.4 0.1 reshape.27.force_ref
  16.5 0.1 pad.1.clone
  16.6 0.0 copy-done.7
  16.6 0.1 fusion
  16.6 0.1 reshape.28
  16.7 0.0 copy-done
  16.7 0.0 copy-start.1
  16.7 1.4 copy-done.1
  18.1 0.9 copy-done.2
  19.1 0.9 copy-done.3
  20.0 154.8 %shard_map.91 = f32[2,8,64,128]{3,2,1,0:T(8,128)S(1)} custom-call(f32[2,8,64,128]{3,2,1,0:T(8,128)S(1)} %reshape.25.source_ref, f32[3,2,128]{2,1,0:T(2,128)S(1)} %reshape.26.geom_ref, f32[2,128]{1,0:T(2,128)S(1)} %reshape.27.force_ref, f32[1,384]{1,0:T(1,128)S(1)} %fusion.1.live_ref, f32[288,2048]{1,0:T(8,128)S(1)} %bitcast.17, ...), custom_call_target="tpu_custom_call" | custom-call | tf_op jit(solution)/shard_map/pallas_call | solution.py:585
  174.8 0.9 reshape.30
  175.7 4.8 %copy.14 = f32[2,8,8,8,4,32]{3,5,2,4,0,1:T(8,128)} copy(f32[2,8,8,8,4,32]{5,4,3,2,1,0:T(4,128)S(1)} %reshape.30) | data formatting | bytes 1048576 | tf_op jit(solution)/shard_map/reshape | solution.py:628
  180.5 6.9 %reshape.31 = f32[8,8,2,4,256]{4,1,3,2,0:T(8,128)S(1)} reshape(f32[8,8,2,4,32,8]{5,4,1,3,2,0:T(8,128)} %bitcast.19) | data formatting | bytes 1048576 | tf_op jit(solution)/shard_map/reshape | solution.py:629
  187.4 1.0 copy.15
  (11 shorter events, 0.0 us)
Async XLA Ops:
  13.7 2.6 %copy-start.4 = (f32[3,2,4,32]{3,2,1,0:T(4,128)S(1)}, f32[3,2,4,32]{3,2,1,0:T(4,128)}, u32[]{:S(2)}) copy-start(f32[3,2,4,32]{3,2,1,0:T(4,128)} %param.10) | copy-start | bytes 9220
  13.7 2.7 %copy-start.5 = (f32[2,4,32]{2,1,0:T(4,128)S(1)}, f32[2,4,32]{2,1,0:T(4,128)}, u32[]{:S(2)}) copy-start(f32[2,4,32]{2,1,0:T(4,128)} %param.12) | copy-start | bytes 3076
  13.7 2.7 %copy-start.6 = (s32[2,4,32]{2,1,0:T(4,128)S(1)}, s32[2,4,32]{2,1,0:T(4,128)}, u32[]{:S(2)}) copy-start(s32[2,4,32]{2,1,0:T(4,128)} %param.11) | copy-start | bytes 3076
  13.7 2.9 %copy-start.7 = (s32[9,1]{0,1:T(1,128)S(1)}, s32[9,1]{0,1:T(1,128)}, u32[]{:S(2)}) copy-start(s32[9,1]{0,1:T(1,128)} %param.14) | copy-start | bytes 112
  13.7 3.1 %copy-start = (f32[9,32,2048]{2,1,0:T(8,128)S(1)}, f32[9,32,2048]{2,1,0:T(8,128)}, u32[]{:S(2)}) copy-start(f32[9,32,2048]{2,1,0:T(8,128)} %param.13) | copy-start | bytes 7077892
  16.7 1.4 copy-start.1
  18.1 0.9 copy-start.2
  19.1 0.9 copy-start.3
where the time goes:
time: 189 us; the launch traced here: 188 us
  Pallas kernels  155 us (82%)
  local copies, waits for them, and re-layouts  33.5 us (18%)
    pallas_call x1, Pallas kernels, per_device(): pl.pallas_call(functools.partial(kernel, n_gx, n_gy, levels, interp), out...  155 us
    reshape x2, local copies, waits for them, and re-layouts, per_device(): return out.reshape(source.shape)  7.93 us
    transpose x1, local copies, waits for them, and re-layouts, per_device(): nodes = nodes.transpose(2, 0, 1, 5, 3, 4).reshape(EX, NODES, 64, LANES)  6.28 us
    reshape x1, local copies, waits for them, and re-layouts, per_device(): nodes = source.reshape(NODES, NODES, EX, EY, EZ, NODES)  6.17 us
    reshape x2, local copies, waits for them, and re-layouts, per_device(): out.reshape(EX, NODES, NODES, NODES, EY, EZ).transpose(1, 2, 0, 4, 5, 3)  5.67 us
    unnamed x17, local copies, waits for them, and re-layouts  4.49 us

commit v1 on v0

--- a/solution.py
+++ b/solution.py
@@ -81,7 +81,7 @@
     eigen_values, eigen_vectors = jacobi_eigen(symmetric)
     eigen_modes = root_inverse[:, None] * eigen_vectors
     vertex_interp = np.stack([(1.0 - points) / 2.0, (1.0 + points) / 2.0], axis=1)
-    return weights, eigen_modes, eigen_values, vertex_interp
+    return weights, stiffness, eigen_modes, eigen_values, vertex_interp
 
 
 def mode_order(modes):
@@ -98,7 +98,7 @@
 
 
 def constant_tables():
-    weights, modes, values, interp = gll_tables(NODES)
+    weights, stiffness, modes, values, interp = gll_tables(NODES)
     even, odd = mode_order(modes)
     half = NODES // 2
     mats = []
@@ -106,6 +106,8 @@
         inverse = np.kron(modes[:half][:, chosen], np.kron(modes, modes))
         mats.append((split_pair(inverse.T), split_pair(inverse)))
     matrices = np.stack([mats[0][0], mats[1][0], mats[0][1], mats[1][1]])
+    plane = np.kron(modes, modes)
+    plane_matrices = np.stack([split_pair(plane.T), split_pair(plane)])
     full = np.ones((NODES, LANES))
     edge = np.ones(NODES)
     edge[0] = edge[-1] = 0.5
@@ -119,13 +121,26 @@
     rows += [value * full for value in edge]
     rows += [values[:, None] * full, weights[:, None] * full, free / z_shared, free * full]
     rows += [interp[:, 0:1] * full, interp[:, 1:2] * full]
+    rows += [stiffness[:, c : c + 1] * full for c in range(NODES)]
     table = np.stack(rows).astype(np.float32)
     perm = np.zeros((2 * LANES, 2 * LANES), np.float32)
     for t in range(2):
         for element in range(LANES):
             perm[t * LANES + element, 2 * element + t] = 1.0
-    perms = np.stack([perm, perm.T]).astype(ml_dtypes.bfloat16)
-    return matrices, table, perms, interp.astype(np.float32)
+    order = np.zeros((EZ * NODES, EZ * NODES), np.float32)
+    for c in range(NODES):
+        for element in range(EZ):
+            order[element * NODES + c, c * EZ + element] = 1.0
+    perms = np.stack([perm, perm.T, order, order.T]).astype(ml_dtypes.bfloat16)
+    return (
+        matrices,
+        plane_matrices,
+        table,
+        perms,
+        interp.astype(np.float32),
+        stiffness.astype(np.float32),
+        weights.astype(np.float32),
+    )
 
 
 def flipped(index, bits):
@@ -155,39 +170,58 @@
     n_gy,
     levels,
     interp,
+    stiff,
+    weights,
     source_ref,
     geom_ref,
     force_ref,
     live_ref,
-    x_factor_ref,
-    mat_ref,
+    x_hbm,
+    mat_hbm,
+    plane_ref,
     tab_ref,
     perm_ref,
     out_ref,
     u_ref,
     r_ref,
     d_ref,
+    x_ref,
     weight_ref,
     winv_ref,
     lam_ref,
     inv_ref,
+    face_lam,
+    face_normal,
+    line_tab,
+    x_factor_ref,
+    mat_ref,
     send_x,
     send_y,
     send_c,
     recv_x,
     recv_y,
     recv_c,
+    recv_g,
     send_one,
     recv_one,
     send_two,
     recv_two,
     send_sem,
     recv_sem,
+    g_send_sem,
+    g_recv_sem,
     one_send_sem,
     one_recv_sem,
     two_send_sem,
     two_recv_sem,
+    load_sem,
 ):
+    loads = [
+        pltpu.make_async_copy(mat_hbm, mat_ref, load_sem.at[0]),
+        pltpu.make_async_copy(x_hbm, x_factor_ref, load_sem.at[1]),
+    ]
+    for load in loads:
+        load.start()
     me_x = lax.axis_index("gx")
     me_y = lax.axis_index("gy")
     left = lax.rem(me_x + n_gx - 1, n_gx)
@@ -204,6 +238,8 @@
         (left, up),
         (right, down),
     ]
+    FROM_RIGHT, FROM_LEFT, FROM_UP, FROM_DOWN = 0, 1, 2, 3
+    FROM_RIGHT_UP, FROM_LEFT_DOWN, FROM_RIGHT_DOWN, FROM_LEFT_UP = 4, 5, 6, 7
     one_targets = [(me_x, flipped(me_y, off)) for off in range(1, n_gy)]
     two_targets = [(flipped(me_x, off), me_y) for off in range(1, n_gx)]
     barrier = pltpu.get_barrier_semaphore()
@@ -214,7 +250,7 @@
     lane = lax.broadcasted_iota(jnp.int32, (1, 1, 1, LANES), 3)
     lane3 = lax.broadcasted_iota(jnp.int32, (1, 1, LANES), 2)
     lane2 = lax.broadcasted_iota(jnp.int32, (1, LANES), 1)
-    ez = lax.rem(lane, EZ)
+    z2 = lax.rem(lane2, EZ)
 
     def roll(value, shift):
         shift = shift % LANES
@@ -228,15 +264,46 @@
     w_c = tab_ref[33]
     zmask = tab_ref[34]
     free = tab_ref[35]
+    w_end = float(weights[0])
+    k_end = float(stiff[0, 0])
     weight_ref[...] = (w_node[:, None] * w_node[None] * w_c[None, None]).reshape(8, 64, LANES)
     winv_ref[...] = (edge[:, None] * edge[None] * zmask[None, None]).reshape(8, 64, LANES)
+
+    def metrics(hx, hy, hz):
+        return hy * hz / (2.0 * hx), hx * hz / (2.0 * hy), hx * hy / (2.0 * hz)
+
+    for half in range(2):
+        at = slice(half * LANES, (half + 1) * LANES)
+        d_ref[half] = source_ref[:, at].reshape(8, 64, LANES)
+    by_node = exact_rows(
+        jnp.concatenate(
+            [
+                jnp.concatenate(
+                    [d_ref[half, a, pl.ds(k, 8, stride=8)] for half in range(2)], axis=1
+                )
+                for k in range(EX * EY)
+                for a in range(NODES)
+            ],
+            axis=0,
+        ),
+        perm_ref[2],
+    )
     for ex in range(EX):
-        hx = geom_ref[0, ex : ex + 1]
-        hy = geom_ref[1, ex : ex + 1]
-        hz = geom_ref[2, ex : ex + 1]
-        ax = hy * hz / (2.0 * hx)
-        ay = hx * hz / (2.0 * hy)
-        az = hx * hy / (2.0 * hz)
+        for c in range(NODES):
+            at = slice(c // 4 * LANES, (c // 4 + 1) * LANES)
+            joined = None
+            for ey in range(EY):
+                first = (ex * EY + ey) * 64
+                part = roll(by_node[first : first + 64, at], EZ * (ey - c % 4))
+                joined = part if ey == 0 else jnp.where(lane2 >= EZ * ey, part, joined)
+            for a in range(NODES):
+                u_ref[ex, a, pl.ds(c, 8, stride=8)] = joined[8 * a : 8 * a + 8]
+
+    for ex in range(EX):
+        hx = geom_ref[ex : ex + 1]
+        hy = geom_ref[2 + ex : 3 + ex]
+        hz = geom_ref[4 + ex : 5 + ex]
+        ax, ay, az = metrics(hx, hy, hz)
         in_x = lam_i * ax[None]
         in_y = lam_j * ay[None]
         in_z = lam_k * az
@@ -245,7 +312,7 @@
         lam_ref[ex] = spectrum
         inv_ref[ex] = 1.0 / (spectrum + shift[None])
         mass = (hx * hy * hz / 8.0)[None] * weight_ref[...]
-        u_ref[ex] = mass * (source_ref[ex] + force_ref[ex : ex + 1][None])
+        u_ref[ex] = mass * (u_ref[ex] + force_ref[ex : ex + 1][None])
 
     def free_scaled(value):
         return (value.reshape(8, 8, 8, LANES) * free[None, None]).reshape(8, 64, LANES)
@@ -255,7 +322,20 @@
 
     pl.semaphore_wait(barrier, len(everyone))
 
-    def assemble(slot):
+    geom_copies = []
+    for index, target in enumerate(targets):
+        copy = pltpu.make_async_remote_copy(
+            src_ref=geom_ref,
+            dst_ref=recv_g.at[index],
+            send_sem=g_send_sem.at[index],
+            recv_sem=g_recv_sem.at[index],
+            device_id=target,
+            device_id_type=MESH,
+        )
+        copy.start()
+        geom_copies.append(copy)
+
+    def own_pairs():
         shared = u_ref[0, 7] + u_ref[1, 0]
         u_ref[0, 7] = shared
         u_ref[1, 0] = shared
@@ -267,34 +347,69 @@
             for a in range(NODES):
                 low = u_ref[ex, a, pl.ds(0, 8, stride=8)]
                 high = u_ref[ex, a, pl.ds(7, 8, stride=8)]
-                z2 = lax.rem(lane2, EZ)
                 u_ref[ex, a, pl.ds(0, 8, stride=8)] = low + jnp.where(
                     z2 > 0, roll(high, 1), 0.0
                 )
                 u_ref[ex, a, pl.ds(7, 8, stride=8)] = high + jnp.where(
                     z2 < EZ - 1, roll(low, -1), 0.0
                 )
-        send_x[slot, 0] = u_ref[0, 0]
-        send_x[slot, 1] = u_ref[1, 7]
-        send_c[slot, 0] = u_ref[0, 0, 0:8]
-        send_c[slot, 1] = u_ref[1, 7, 56:64]
-        send_c[slot, 2] = u_ref[0, 0, 56:64]
-        send_c[slot, 3] = u_ref[1, 7, 0:8]
-        for ex in range(EX):
-            for which, first, ey in ((0, 0, 0), (1, 56, EY - 1)):
-                packed = None
-                for s in range(4):
-                    face = roll(
-                        u_ref[ex, 2 * s : 2 * s + 2, first : first + 8], EZ * (s - ey)
-                    )
-                    packed = (
-                        face if packed is None else jnp.where(lane3 >= EZ * s, face, packed)
-                    )
-                send_y[slot, which, ex] = packed
+
+    def packed_y(down_faces, up_faces):
+        return jnp.where(
+            lane3 < EZ,
+            down_faces[0],
+            jnp.where(
+                lane3 < 2 * EZ,
+                roll(down_faces[1], EZ),
+                jnp.where(lane3 < 3 * EZ, roll(up_faces[0], -EZ), up_faces[1]),
+            ),
+        )
+
+    def y_faces():
+        return packed_y(
+            [u_ref[ex, :, 0:8] for ex in range(EX)], [u_ref[ex, :, 56:64] for ex in range(EX)]
+        )
+
+    def weighted(parts, row):
+        total = None
+        for index, part in parts:
+            term = part * float(stiff[row, index])
+            total = term if total is None else total + term
+        return total
+
+    def exchange_faces(slot, planes):
+        send_x[slot, 0, 0] = u_ref[0, 0]
+        send_x[slot, 1, 0] = u_ref[1, 7]
+        send_y[slot, 0] = y_faces()
+        send_c[slot, 0, 0] = u_ref[0, 0, 0:8]
+        send_c[slot, 1, 0] = u_ref[1, 7, 56:64]
+        send_c[slot, 2, 0] = u_ref[0, 0, 56:64]
+        send_c[slot, 3, 0] = u_ref[1, 7, 0:8]
+        if planes > 1:
+            low = weighted([(a, u_ref[0, a]) for a in range(1, NODES)], 0)
+            high = weighted([(a, u_ref[1, a]) for a in range(NODES - 1)], 7)
+            send_x[slot, 0, 1] = low
+            send_x[slot, 1, 1] = high
+            send_c[slot, 0, 1] = low[0:8]
+            send_c[slot, 1, 1] = high[56:64]
+            send_c[slot, 2, 1] = low[56:64]
+            send_c[slot, 3, 1] = high[0:8]
+            down_normal, up_normal = [], []
+            for ex in range(EX):
+                rows = [u_ref[ex, :, 8 * b : 8 * b + 8] for b in range(NODES)]
+                down_normal.append(weighted([(b, rows[b]) for b in range(1, NODES)], 0))
+                up_normal.append(weighted([(b, rows[b]) for b in range(NODES - 1)], 7))
+            normal = packed_y(down_normal, up_normal)
+            send_y[slot, 1] = normal
+            send_c[slot, 0, 2] = normal[0]
+            send_c[slot, 1, 2] = normal[7]
+            send_c[slot, 2, 2] = normal[0]
+            send_c[slot, 3, 2] = normal[7]
+        lines = 3 if planes > 1 else 1
         pairs = (
-            [(send_x.at[slot, i], recv_x.at[slot, i]) for i in range(2)]
-            + [(send_y.at[slot, i], recv_y.at[slot, i]) for i in range(2)]
-            + [(send_c.at[slot, i], recv_c.at[slot, i]) for i in range(4)]
+            [(send_x.at[slot, i, pl.ds(0, planes)], recv_x.at[slot, i, pl.ds(0, planes)]) for i in range(2)]
+            + [(send_y.at[slot, pl.ds(0, planes)], recv_y.at[slot, i, pl.ds(0, planes)]) for i in range(2)]
+            + [(send_c.at[slot, i, pl.ds(0, lines)], recv_c.at[slot, i, pl.ds(0, lines)]) for i in range(4)]
         )
         copies = []
         for index, (source, landing) in enumerate(pairs):
@@ -310,16 +425,9 @@
             copies.append(copy)
         for copy in copies:
             copy.wait()
-        u_ref[1, 7] += recv_x[slot, 0]
-        u_ref[0, 0] += recv_x[slot, 1]
-        for ex in range(EX):
-            for which, first, ey in ((0, 56, EY - 1), (1, 0, 0)):
-                packed = recv_y[slot, which, ex]
-                inside = (lane3 >= EZ * ey) & (lane3 < EZ * (ey + 1))
-                for s in range(4):
-                    u_ref[ex, 2 * s : 2 * s + 2, first : first + 8] += jnp.where(
-                        inside, roll(packed, EZ * (ey - s)), 0.0
-                    )
+        u_ref[1, 7] += recv_x[slot, FROM_RIGHT, 0]
+        u_ref[0, 0] += recv_x[slot, FROM_LEFT, 0]
+        add_y(arrived_y(slot, 0))
         for index, (ex, a, first, to_ey, from_ey) in enumerate(
             (
                 (1, 7, 56, EY - 1, 0),
@@ -330,8 +438,101 @@
         ):
             inside = (lane2 >= EZ * to_ey) & (lane2 < EZ * (to_ey + 1))
             u_ref[ex, a, first : first + 8] += jnp.where(
-                inside, roll(recv_c[slot, index], EZ * (to_ey - from_ey)), 0.0
-            )
+                inside, roll(recv_c[slot, index, 0], EZ * (to_ey - from_ey)), 0.0
+            )
+
+    def arrived_y(slot, plane):
+        from_up = recv_y[slot, FROM_UP - 2, plane]
+        from_down = recv_y[slot, FROM_DOWN - 2, plane]
+        return roll(jnp.where(lane3 >= 2 * EZ, from_down, from_up), 2 * EZ)
+
+    def add_y(plane):
+        for ex in range(EX):
+            u_ref[ex, :, 0:8] += jnp.where(lane3 < EZ, roll(plane, -EZ * ex), 0.0)
+            u_ref[ex, :, 56:64] += jnp.where(
+                lane3 >= 3 * EZ, roll(plane, EZ * (1 - ex)), 0.0
+            )
+
+    def in_slot(value, slot):
+        return jnp.where((lane2 >= EZ * slot) & (lane2 < EZ * (slot + 1)), value, 0.0)
+
+    def outer_terms(slot):
+        face = jnp.concatenate(
+            [u_ref[0, 0], u_ref[1, 7], y_faces().reshape(64, LANES)], axis=1
+        )
+        from_left_down = recv_c[slot, FROM_LEFT_DOWN - 4]
+        from_left_up = recv_c[slot, FROM_LEFT_UP - 4]
+        from_right_down = recv_c[slot, FROM_RIGHT_DOWN - 4]
+        from_right_up = recv_c[slot, FROM_RIGHT_UP - 4]
+        sides = []
+        for plane, low, high in (
+            (recv_x[slot, FROM_LEFT, 1], from_left_down, from_left_up),
+            (recv_x[slot, FROM_RIGHT, 1], from_right_down, from_right_up),
+        ):
+            sides.append(
+                jnp.concatenate(
+                    [
+                        plane[0:8] + in_slot(roll(low[1], EZ), 0),
+                        plane[8:56],
+                        plane[56:64] + in_slot(roll(high[1], -EZ), 3),
+                    ],
+                    axis=0,
+                )
+            )
+        normal_y = arrived_y(slot, 1)
+        first = (
+            normal_y[0]
+            + in_slot(roll(from_left_down[2], EZ), 0)
+            + in_slot(roll(from_left_up[2], EZ), 2)
+        )
+        last = (
+            normal_y[7]
+            + in_slot(roll(from_right_down[2], -EZ), 1)
+            + in_slot(roll(from_right_up[2], -EZ), 3)
+        )
+        normal_y = jnp.concatenate([first[None], normal_y[1:7], last[None]], axis=0)
+        normal = jnp.concatenate([sides[0], sides[1], normal_y.reshape(64, LANES)], axis=1)
+        weight = weight_ref[0] * (1.0 / w_end)
+        weight = jnp.concatenate([weight] * 3, axis=1)
+        spread = small_product(1, face_lam[...] * small_product(0, weight * face))
+        result = face_normal[...] * (normal + k_end * face) + w_end * weight * spread
+        lines = []
+        for side in range(2):
+            plane = face[:, side * LANES : (side + 1) * LANES]
+            value = jnp.where(lane2 < 2 * EZ, plane[0:8], plane[56:64])
+            along_x = jnp.where(lane2 < 2 * EZ, sides[side][0:8], sides[side][56:64])
+            edge_y = last if side else first
+            along_y = jnp.where(
+                lane2 < 2 * EZ,
+                roll(edge_y, -EZ) if side else edge_y,
+                edge_y if side else roll(edge_y, EZ),
+            )
+            along_z = None
+            for c in range(NODES):
+                term = tab_ref[38 + c] * value[c : c + 1]
+                along_z = term if along_z is None else along_z + term
+            lines.append(
+                line_tab[side, 0] * (along_x + k_end * value)
+                + line_tab[side, 1] * (along_y + k_end * value)
+                + line_tab[side, 2] * along_z
+            )
+        return result, lines
+
+    def add_outer(result, lines):
+        for side, (ex, a) in enumerate(((0, 0), (1, 7))):
+            u_ref[ex, a] += result[:, side * LANES : (side + 1) * LANES]
+            u_ref[ex, a, 0:8] += in_slot(lines[side], 0)
+            u_ref[ex, a, 56:64] += in_slot(lines[side], 3)
+        add_y(result[:, 2 * LANES :].reshape(8, 8, LANES))
+
+    def small_product(which, value):
+        high = value.astype(jnp.bfloat16)
+        low = (value - high.astype(jnp.float32)).astype(jnp.bfloat16)
+        return jnp.dot(
+            plane_ref[which],
+            jnp.concatenate([high, low, high], axis=0),
+            preferred_element_type=jnp.float32,
+        )
 
     def product(which, value):
         high = value.astype(jnp.bfloat16)
@@ -369,14 +570,14 @@
 
     def stiffness():
         weight = weight_ref[...]
-        out = element_op([d_ref[ex] * weight for ex in range(EX)], lam_ref)
+        out = element_op([u_ref[ex] * weight for ex in range(EX)], lam_ref)
         for ex in range(EX):
-            u_ref[ex] = free_scaled(out[ex] * weight)
-
-    def smoother():
+            u_ref[ex] = out[ex] * weight
+
+    def smoother(keep, take):
         out = element_op([r_ref[ex] for ex in range(EX)], inv_ref)
         for ex in range(EX):
-            u_ref[ex] = out[ex] * winv_ref[...]
+            u_ref[ex] = (take * out[ex] + keep * d_ref[ex]) * winv_ref[...]
 
     wide = (levels - 1) * XCOLS
     gy_bits = n_gy.bit_length() - 1
@@ -413,15 +614,6 @@
         return total
 
     def coarse(cycle):
-        columns = []
-        for t in range(2):
-            to_t = tab_ref[36 + t]
-            rows = []
-            for v in range(2):
-                for u in range(2):
-                    for ex in range(EX):
-                        rows.append((v, u, ex))
-            columns.append(rows)
         sums = {}
         for ex in range(EX):
             scaled = r_ref[ex] * winv_ref[...]
@@ -520,19 +712,65 @@
     rho_old = 1.0 / ratio
     rho_new = 1.0 / (2.0 * ratio - rho_old)
 
-    assemble(1)
+    own_pairs()
+    exchange_faces(1, 1)
     r_ref[...] = u_ref[...]
     d_ref[...] = jnp.zeros_like(d_ref)
-    out_ref[...] = jnp.zeros_like(out_ref)
+    x_ref[...] = jnp.zeros_like(x_ref)
+
+    for copy in geom_copies:
+        copy.wait()
+    slots = lambda values: jnp.where(
+        lane2 < EZ,
+        values[0],
+        jnp.where(lane2 < 2 * EZ, values[1], jnp.where(lane2 < 3 * EZ, values[2], values[3])),
+    )
+
+    def ghost(source, dim, ex):
+        return recv_g[source, 2 * dim + ex : 2 * dim + ex + 1]
+
+    outer = []
+    for dim in range(3):
+        y_side = slots(
+            [
+                roll(ghost(FROM_DOWN, dim, 0), EZ),
+                roll(ghost(FROM_DOWN, dim, 1), 2 * EZ),
+                roll(ghost(FROM_UP, dim, 0), 2 * EZ),
+                roll(ghost(FROM_UP, dim, 1), 3 * EZ),
+            ]
+        )
+        outer.append([ghost(FROM_LEFT, dim, 1), ghost(FROM_RIGHT, dim, 0), y_side])
+    for part in range(3):
+        ax, ay, az = metrics(*[outer[dim][part] for dim in range(3)])
+        at = slice(part * LANES, (part + 1) * LANES)
+        normal, along = (ay, ax) if part == 2 else (ax, ay)
+        face_lam[:, at] = ((lam_j * along[None]) + (lam_k * az)[None]).reshape(64, LANES)
+        face_normal[:, at] = (w_node * w_c[None] * normal[None]).reshape(64, LANES)
+    for side, (low, high, ex) in enumerate(
+        ((FROM_LEFT_DOWN, FROM_LEFT_UP, 1), (FROM_RIGHT_DOWN, FROM_RIGHT_UP, 0))
+    ):
+        lengths = [
+            jnp.where(
+                lane2 < 2 * EZ,
+                roll(ghost(low, dim, ex), EZ),
+                roll(ghost(high, dim, ex), -EZ),
+            )
+            for dim in range(3)
+        ]
+        ax, ay, az = metrics(*lengths)
+        line_tab[side, 0] = w_end * w_c * ax
+        line_tab[side, 1] = w_end * w_c * ay
+        line_tab[side, 2] = jnp.broadcast_to(w_end * w_end * az, (8, LANES))
+
+    for load in loads:
+        load.wait()
 
     def step(index, carry):
         phase = lax.rem(index, SMOOTH)
         cycle = lax.div(index, SMOOTH)
+        slot = lax.rem(index, 2)
         is_coarse = phase == 2
         second = (phase == 1) | (phase == 4)
-        keep = jnp.where(second, rho_new * rho_old, 0.0)
-        take = jnp.where(second, 2.0 * rho_new / radius, 1.0 / center)
-        take = jnp.where(is_coarse, 1.0, take)
 
         @pl.when(is_coarse)
         def _():
@@ -540,24 +778,59 @@
 
         @pl.when(jnp.logical_not(is_coarse))
         def _():
-            smoother()
-
-        assemble(0)
+            keep = jnp.where(second, rho_new * rho_old, 0.0)
+            take = jnp.where(second, 2.0 * rho_new / radius, 1.0 / center)
+            smoother(keep, take)
+
+        own_pairs()
+        exchange_faces(slot, 2)
         for ex in range(EX):
-            direction = keep * d_ref[ex] + take * u_ref[ex]
-            d_ref[ex] = direction
-            out_ref[ex] += direction
+            d_ref[ex] = u_ref[ex]
+            x_ref[ex] += u_ref[ex]
 
         @pl.when(index < SMOOTH * CYCLES - 1)
         def _():
+            result, lines = outer_terms(slot)
             stiffness()
-            assemble(1)
+            add_outer(result, lines)
+            own_pairs()
             for ex in range(EX):
-                r_ref[ex] -= u_ref[ex]
+                r_ref[ex] -= free_scaled(u_ref[ex])
 
         return carry
 
     lax.fori_loop(0, SMOOTH * CYCLES, step, 0)
+
+    by_node = [
+        [
+            jnp.concatenate(
+                [x_ref[ex, a, pl.ds(c, 8, stride=8)] for a in range(NODES)], axis=0
+            )
+            for c in range(NODES)
+        ]
+        for ex in range(EX)
+    ]
+    rows = []
+    for ex in range(EX):
+        for ey in range(EY):
+            halves = []
+            for half in range(2):
+                joined = None
+                for s in range(4):
+                    part = roll(by_node[ex][half * 4 + s], EZ * (s - ey))
+                    joined = part if s == 0 else jnp.where(lane2 >= EZ * s, part, joined)
+                halves.append(joined)
+            rows.append(jnp.concatenate(halves, axis=1))
+    result = exact_rows(jnp.concatenate(rows, axis=0), perm_ref[3])
+    for half in range(2):
+        at = slice(half * LANES, (half + 1) * LANES)
+        for k in range(EX * EY):
+            for a in range(NODES):
+                first = k * 64 + a * 8
+                d_ref[half, a, pl.ds(k, 8, stride=8)] = result[first : first + 8, at]
+    for half in range(2):
+        at = slice(half * LANES, (half + 1) * LANES)
+        out_ref[:, at] = d_ref[half].reshape(512, LANES)
 
 
 def per_device(source, geometry, disc_mask, thrust, xxt_factor, col_count):
@@ -566,10 +839,10 @@
     levels = xxt_factor.shape[0]
     wide = (levels - 1) * XCOLS
     split = (n_gy.bit_length() - 1) * XCOLS
-    matrices, table, perms, interp = constant_tables()
-    nodes = source.reshape(NODES, NODES, EX, EY, EZ, NODES)
-    nodes = nodes.transpose(2, 0, 1, 5, 3, 4).reshape(EX, NODES, 64, LANES)
-    geom = geometry.reshape(3, EX, LANES)
+    matrices, plane, table, perms, interp, stiff, weights = constant_tables()
+    geom = jnp.concatenate(
+        [geometry.reshape(3 * EX, LANES), jnp.ones((8 - 3 * EX, LANES), jnp.float32)], axis=0
+    )
     force = (disc_mask.astype(jnp.float32) * thrust).reshape(EX, LANES)
     live = (jnp.arange(XCOLS)[None, :] < col_count).astype(jnp.float32)
     live = jnp.concatenate(
@@ -583,11 +856,14 @@
     field = (EX, NODES, 64, LANES)
     f32 = jnp.float32
     out = pl.pallas_call(
-        functools.partial(kernel, n_gx, n_gy, levels, interp),
-        out_shape=jax.ShapeDtypeStruct(field, f32),
-        in_specs=[pl.BlockSpec(memory_space=pltpu.VMEM)] * 8,
+        functools.partial(kernel, n_gx, n_gy, levels, interp, stiff, weights),
+        out_shape=jax.ShapeDtypeStruct((512, 256), f32),
+        in_specs=[pl.BlockSpec(memory_space=pltpu.VMEM)] * 4
+        + [pl.BlockSpec(memory_space=pl.ANY)] * 2
+        + [pl.BlockSpec(memory_space=pltpu.VMEM)] * 3,
         out_specs=pl.BlockSpec(memory_space=pltpu.VMEM),
         scratch_shapes=[
+            pltpu.VMEM(field, f32),
             pltpu.VMEM(field, f32),
             pltpu.VMEM(field, f32),
             pltpu.VMEM(field, f32),
@@ -595,37 +871,46 @@
             pltpu.VMEM(field[1:], f32),
             pltpu.VMEM(field, f32),
             pltpu.VMEM(field, f32),
-            pltpu.VMEM((2, 2, 64, LANES), f32),
-            pltpu.VMEM((2, 2, EX, 2, 8, LANES), f32),
-            pltpu.VMEM((2, 4, 8, LANES), f32),
-            pltpu.VMEM((2, 2, 64, LANES), f32),
-            pltpu.VMEM((2, 2, EX, 2, 8, LANES), f32),
-            pltpu.VMEM((2, 4, 8, LANES), f32),
+            pltpu.VMEM((64, 3 * LANES), f32),
+            pltpu.VMEM((64, 3 * LANES), f32),
+            pltpu.VMEM((2, 3, 8, LANES), f32),
+            pltpu.VMEM((levels * XCOLS, xxt_factor.shape[2]), f32),
+            pltpu.VMEM(matrices.shape, jnp.bfloat16),
+            pltpu.VMEM((2, 2, 2, 64, LANES), f32),
+            pltpu.VMEM((2, 2, 8, 8, LANES), f32),
+            pltpu.VMEM((2, 4, 3, 8, LANES), f32),
+            pltpu.VMEM((2, 2, 2, 64, LANES), f32),
+            pltpu.VMEM((2, 2, 2, 8, 8, LANES), f32),
+            pltpu.VMEM((2, 4, 3, 8, LANES), f32),
+            pltpu.VMEM((8, 8, LANES), f32),
             pltpu.VMEM((1, wide), f32),
             pltpu.VMEM((CYCLES, n_gy - 1, 1, wide), f32),
             pltpu.VMEM((1, wide - split), f32),
             pltpu.VMEM((CYCLES, n_gx - 1, 1, wide - split), f32),
             pltpu.SemaphoreType.DMA((2, 8)),
             pltpu.SemaphoreType.DMA((2, 8)),
+            pltpu.SemaphoreType.DMA((8,)),
+            pltpu.SemaphoreType.DMA((8,)),
             pltpu.SemaphoreType.DMA((n_gy - 1,)),
             pltpu.SemaphoreType.DMA((CYCLES, n_gy - 1)),
             pltpu.SemaphoreType.DMA((n_gx - 1,)),
             pltpu.SemaphoreType.DMA((CYCLES, n_gx - 1)),
+            pltpu.SemaphoreType.DMA((2,)),
         ],
         compiler_params=pltpu.CompilerParams(
             collective_id=0, has_side_effects=True, vmem_limit_bytes=48 * 1024 * 1024
         ),
     )(
-        nodes,
+        source.reshape(NODES * NODES * EX * EY, EZ * NODES),
         geom,
         force,
         live,
         xxt_factor.reshape(levels * XCOLS, xxt_factor.shape[2]),
         jnp.asarray(matrices),
+        jnp.asarray(plane),
         jnp.asarray(table),
         jnp.asarray(perms),
     )
-    out = out.reshape(EX, NODES, NODES, NODES, EY, EZ).transpose(1, 2, 0, 4, 5, 3)
     return out.reshape(source.shape)
 
 

time: 189 us -> 129 us (0.68)
  Pallas kernels: 155 us -> 118 us
  local copies, waits for them, and re-layouts: 33.5 us -> 9.07 us
    pallas_call x1, Pallas kernels: 155 us -> 118 us  [per_device(): pl.pallas_call(functools.partial(kernel, n_gx, n_gy, levels, interp, stif...]
    reshape x5 -> x2, local copies, waits for them, and re-layouts: 14.5 us -> 2.01 us  [the longest x1 1.22 us: per_device(): source.reshape(NODES * NODES * EX * EY, EZ * NODES)]
    reshape x2 -> x1, local copies, waits for them, and re-layouts: 7.93 us -> 0.94 us  [per_device(): return out.reshape(source.shape)]
    transpose x1 -> x0, local copies, waits for them, and re-layouts: 6.28 us -> none  [per_device(): nodes = nodes.transpose(2, 0, 1, 5, 3, 4).reshape(EX, NODES, 64, LANES)]
    unnamed x17 -> x10, local copies, waits for them, and re-layouts: 4.49 us -> 5.87 us
where the time goes in v1:
time: 129 us; the launch traced here: 128 us
  Pallas kernels  118 us (91%)
  local copies, waits for them, and re-layouts  9.07 us (7%)
  other arithmetic  1.44 us (1%)
    pallas_call x1, Pallas kernels, per_device(): pl.pallas_call(functools.partial(kernel, n_gx, n_gy, levels, interp, stif...  118 us
    unnamed x10, local copies, waits for them, and re-layouts  5.87 us

profile of v1, /device:TPU:1, one launch (start us, length us, event | category | flops | bytes accessed | tf_op | source)
XLA Modules:
  0.0 128.2 jit_solution(7475579683230589669)
XLA Ops:
  0.0 0.1 pad.2.clone
  0.1 0.8 reshape.19
  0.9 0.7 convert_multiply_fusion
  1.6 0.1 reshape.20.force_ref
  1.7 0.7 fusion
  2.4 0.1 reshape.21
  2.5 1.2 reshape.18.source_ref
  3.7 0.0 copy-start
  3.7 1.7 %copy-done = f32[9,32,2048]{2,1,0:T(8,128)S(1)} copy-done((f32[9,32,2048]{2,1,0:T(8,128)S(1)}, f32[9,32,2048]{2,1,0:T(8,128)}, u32[]{:S(2)}) %copy-start) | copy-done | bytes 2359320
  5.4 0.0 copy-start.1
  5.4 1.4 %copy-done.1 = bf16[4,256,768]{2,1,0:T(8,128)(2,1)S(1)} copy-done((bf16[4,256,768]{2,1,0:T(8,128)(2,1)S(1)}, bf16[4,256,768]{2,1,0:T(8,128)(2,1)}, u32[]{:S(2)}) %copy-start.1) | copy-done | bytes 1572888
  6.8 0.0 copy-start.2
  6.8 1.0 copy-done.2
  7.8 0.0 copy-start.3
  7.8 0.9 copy-done.3
  8.8 0.0 copy-start.4
  8.8 0.8 copy-done.4
  9.6 117.6 %shard_map.100 = f32[512,256]{1,0:T(8,128)S(1)} custom-call(f32[512,256]{1,0:T(8,128)S(1)} %reshape.18.source_ref, f32[8,128]{1,0:T(8,128)S(1)} %concatenate.6.geom_ref, f32[2,128]{1,0:T(2,128)S(1)} %reshape.20.force_ref, f32[1,384]{1,0:T(1,128)S(1)} %fusion.1.live_ref, f32[288,2048]{1,0:T(8,128)S(1)} %bitcast.5, bf16[4,256,768]{2,1,0:T(8,128)(2,1)S(1)} %copy-done.1, ...), custom_call_target="tpu_custom_call" | custom-call | tf_op jit(solution)/shard_map/pallas_call | solution.py:858
  127.3 0.9 reshape.23
  (5 shorter events, 0.0 us)
Async XLA Ops:
  3.7 1.7 %copy-start = (f32[9,32,2048]{2,1,0:T(8,128)S(1)}, f32[9,32,2048]{2,1,0:T(8,128)}, u32[]{:S(2)}) copy-start(f32[9,32,2048]{2,1,0:T(8,128)} %param.14) | copy-start | bytes 7077892
  5.4 1.4 %copy-start.1 = (bf16[4,256,768]{2,1,0:T(8,128)(2,1)S(1)}, bf16[4,256,768]{2,1,0:T(8,128)(2,1)}, u32[]{:S(2)}) copy-start(bf16[4,256,768]{2,1,0:T(8,128)(2,1)} %constant.12.clone.mat_hbm) | copy-start | bytes 4718596
  6.8 1.0 copy-start.2
  7.8 0.9 copy-start.3
  8.8 0.8 copy-start.4

commit v2 on v1

--- a/solution.py
+++ b/solution.py
@@ -172,16 +172,27 @@
     interp,
     stiff,
     weights,
-    source_ref,
-    geom_ref,
-    force_ref,
-    live_ref,
+    source_hbm,
+    lengths_hbm,
+    disc_hbm,
+    thrust_hbm,
+    count_hbm,
     x_hbm,
     mat_hbm,
+    plane_hbm,
+    tab_hbm,
+    perm_hbm,
+    out_ref,
+    source_ref,
+    lengths_ref,
+    disc_ref,
+    thrust_ref,
+    count_ref,
     plane_ref,
     tab_ref,
     perm_ref,
-    out_ref,
+    geom_ref,
+    live_ref,
     u_ref,
     r_ref,
     d_ref,
@@ -216,12 +227,6 @@
     two_recv_sem,
     load_sem,
 ):
-    loads = [
-        pltpu.make_async_copy(mat_hbm, mat_ref, load_sem.at[0]),
-        pltpu.make_async_copy(x_hbm, x_factor_ref, load_sem.at[1]),
-    ]
-    for load in loads:
-        load.start()
     me_x = lax.axis_index("gx")
     me_y = lax.axis_index("gy")
     left = lax.rem(me_x + n_gx - 1, n_gx)
@@ -246,6 +251,26 @@
     everyone = targets + one_targets + two_targets
     for target in everyone:
         pl.semaphore_signal(barrier, inc=1, device_id=target, device_id_type=MESH)
+    loads = [
+        pltpu.make_async_copy(src, dst, load_sem.at[index])
+        for index, (src, dst) in enumerate(
+            (
+                (tab_hbm, tab_ref),
+                (source_hbm, source_ref),
+                (perm_hbm, perm_ref),
+                (lengths_hbm, lengths_ref),
+                (disc_hbm, disc_ref),
+                (thrust_hbm, thrust_ref),
+                (count_hbm, count_ref),
+                (mat_hbm, mat_ref),
+                (plane_hbm, plane_ref),
+                (x_hbm, x_factor_ref),
+            )
+        )
+    ]
+    for load in loads:
+        load.start()
+    first_loads, later_loads = loads[:7], loads[7:]
 
     lane = lax.broadcasted_iota(jnp.int32, (1, 1, 1, LANES), 3)
     lane3 = lax.broadcasted_iota(jnp.int32, (1, 1, LANES), 2)
@@ -256,6 +281,29 @@
         shift = shift % LANES
         return value if shift == 0 else pltpu.roll(value, shift, value.ndim - 1)
 
+    for load in first_loads:
+        load.wait()
+    for dim in range(3):
+        for ex in range(EX):
+            geom_ref[2 * dim + ex : 2 * dim + ex + 1] = jnp.concatenate(
+                [lengths_ref[dim, ex, ey : ey + 1] for ey in range(EY)], axis=1
+            )
+    geom_ref[6:8] = jnp.ones((2, LANES), jnp.float32)
+    forces = []
+    for ex in range(EX):
+        element = disc_ref[ex].astype(jnp.float32) * thrust_ref[ex]
+        forces.append(
+            jnp.concatenate([element[ey : ey + 1] for ey in range(EY)], axis=1)
+        )
+    column = lax.rem(lane2, XCOLS)
+    for first in range(0, levels, LANES // XCOLS):
+        chosen = [0] * 4 if first == 0 else range(first - 3, first + 1)
+        count = None
+        for place, level in enumerate(chosen):
+            one = jnp.broadcast_to(count_ref[level : level + 1], (1, LANES))
+            count = one if count is None else jnp.where(lane2 >= XCOLS * place, one, count)
+        at = slice(first // 4 * LANES, (first // 4 + 1) * LANES)
+        live_ref[:, at] = (column < count).astype(jnp.float32)
     lam_i = tab_ref[0:8]
     lam_j = tab_ref[8:16]
     w_node = tab_ref[16:24]
@@ -312,7 +360,7 @@
         lam_ref[ex] = spectrum
         inv_ref[ex] = 1.0 / (spectrum + shift[None])
         mass = (hx * hy * hz / 8.0)[None] * weight_ref[...]
-        u_ref[ex] = mass * (u_ref[ex] + force_ref[ex : ex + 1][None])
+        u_ref[ex] = mass * (u_ref[ex] + forces[ex][None])
 
     def free_scaled(value):
         return (value.reshape(8, 8, 8, LANES) * free[None, None]).reshape(8, 64, LANES)
@@ -381,19 +429,18 @@
         send_x[slot, 0, 0] = u_ref[0, 0]
         send_x[slot, 1, 0] = u_ref[1, 7]
         send_y[slot, 0] = y_faces()
-        send_c[slot, 0, 0] = u_ref[0, 0, 0:8]
-        send_c[slot, 1, 0] = u_ref[1, 7, 56:64]
-        send_c[slot, 2, 0] = u_ref[0, 0, 56:64]
-        send_c[slot, 3, 0] = u_ref[1, 7, 0:8]
+        corners = (
+            (u_ref[0, 0, 0:8], 0),
+            (u_ref[1, 7, 56:64], EY - 1),
+            (u_ref[0, 0, 56:64], EY - 1),
+            (u_ref[1, 7, 0:8], 0),
+        )
+        lines = [roll(value, -EZ * ey) for value, ey in corners]
         if planes > 1:
             low = weighted([(a, u_ref[0, a]) for a in range(1, NODES)], 0)
             high = weighted([(a, u_ref[1, a]) for a in range(NODES - 1)], 7)
             send_x[slot, 0, 1] = low
             send_x[slot, 1, 1] = high
-            send_c[slot, 0, 1] = low[0:8]
-            send_c[slot, 1, 1] = high[56:64]
-            send_c[slot, 2, 1] = low[56:64]
-            send_c[slot, 3, 1] = high[0:8]
             down_normal, up_normal = [], []
             for ex in range(EX):
                 rows = [u_ref[ex, :, 8 * b : 8 * b + 8] for b in range(NODES)]
@@ -401,18 +448,36 @@
                 up_normal.append(weighted([(b, rows[b]) for b in range(NODES - 1)], 7))
             normal = packed_y(down_normal, up_normal)
             send_y[slot, 1] = normal
-            send_c[slot, 0, 2] = normal[0]
-            send_c[slot, 1, 2] = normal[7]
-            send_c[slot, 2, 2] = normal[0]
-            send_c[slot, 3, 2] = normal[7]
-        lines = 3 if planes > 1 else 1
+            along_x = (low[0:8], high[56:64], low[56:64], high[0:8])
+            along_y = ((normal[0], 0), (normal[7], 3), (normal[0], 2), (normal[7], 1))
+            lines = [
+                jnp.where(
+                    lane2 < EZ,
+                    lines[i],
+                    jnp.where(
+                        lane2 < 2 * EZ,
+                        roll(along_x[i], EZ * (1 - corners[i][1])),
+                        roll(along_y[i][0], EZ * (2 - along_y[i][1])),
+                    ),
+                )
+                for i in range(4)
+            ]
+        for i in range(4):
+            send_c[slot, i] = lines[i]
         pairs = (
-            [(send_x.at[slot, i, pl.ds(0, planes)], recv_x.at[slot, i, pl.ds(0, planes)]) for i in range(2)]
-            + [(send_y.at[slot, pl.ds(0, planes)], recv_y.at[slot, i, pl.ds(0, planes)]) for i in range(2)]
-            + [(send_c.at[slot, i, pl.ds(0, lines)], recv_c.at[slot, i, pl.ds(0, lines)]) for i in range(4)]
+            [
+                (send_x.at[slot, i, pl.ds(0, planes)], recv_x.at[slot, i, pl.ds(0, planes)])
+                for i in range(2)
+            ]
+            + [
+                (send_y.at[slot, pl.ds(0, planes)], recv_y.at[slot, i, pl.ds(0, planes)])
+                for i in range(2)
+            ]
+            + [(send_c.at[slot, i], recv_c.at[slot, i]) for i in range(4)]
         )
         copies = []
-        for index, (source, landing) in enumerate(pairs):
+        for index in (4, 5, 6, 7, 0, 1, 2, 3):
+            source, landing = pairs[index]
             copy = pltpu.make_async_remote_copy(
                 src_ref=source,
                 dst_ref=landing,
@@ -428,17 +493,11 @@
         u_ref[1, 7] += recv_x[slot, FROM_RIGHT, 0]
         u_ref[0, 0] += recv_x[slot, FROM_LEFT, 0]
         add_y(arrived_y(slot, 0))
-        for index, (ex, a, first, to_ey, from_ey) in enumerate(
-            (
-                (1, 7, 56, EY - 1, 0),
-                (0, 0, 0, 0, EY - 1),
-                (1, 7, 0, 0, EY - 1),
-                (0, 0, 56, EY - 1, 0),
-            )
+        for index, (ex, a, first, to_ey) in enumerate(
+            ((1, 7, 56, EY - 1), (0, 0, 0, 0), (1, 7, 0, 0), (0, 0, 56, EY - 1))
         ):
-            inside = (lane2 >= EZ * to_ey) & (lane2 < EZ * (to_ey + 1))
-            u_ref[ex, a, first : first + 8] += jnp.where(
-                inside, roll(recv_c[slot, index, 0], EZ * (to_ey - from_ey)), 0.0
+            u_ref[ex, a, first : first + 8] += in_slot(
+                roll(recv_c[slot, index], EZ * to_ey), to_ey
             )
 
     def arrived_y(slot, plane):
@@ -472,9 +531,9 @@
             sides.append(
                 jnp.concatenate(
                     [
-                        plane[0:8] + in_slot(roll(low[1], EZ), 0),
+                        plane[0:8] + in_slot(roll(low, -EZ), 0),
                         plane[8:56],
-                        plane[56:64] + in_slot(roll(high[1], -EZ), 3),
+                        plane[56:64] + in_slot(roll(high, 2 * EZ), 3),
                     ],
                     axis=0,
                 )
@@ -482,13 +541,13 @@
         normal_y = arrived_y(slot, 1)
         first = (
             normal_y[0]
-            + in_slot(roll(from_left_down[2], EZ), 0)
-            + in_slot(roll(from_left_up[2], EZ), 2)
+            + in_slot(roll(from_left_down, -2 * EZ), 0)
+            + in_slot(from_left_up, 2)
         )
         last = (
             normal_y[7]
-            + in_slot(roll(from_right_down[2], -EZ), 1)
-            + in_slot(roll(from_right_up[2], -EZ), 3)
+            + in_slot(roll(from_right_down, -EZ), 1)
+            + in_slot(roll(from_right_up, EZ), 3)
         )
         normal_y = jnp.concatenate([first[None], normal_y[1:7], last[None]], axis=0)
         normal = jnp.concatenate([sides[0], sides[1], normal_y.reshape(64, LANES)], axis=1)
@@ -762,7 +821,7 @@
         line_tab[side, 1] = w_end * w_c * ay
         line_tab[side, 2] = jnp.broadcast_to(w_end * w_end * az, (8, LANES))
 
-    for load in loads:
+    for load in later_loads:
         load.wait()
 
     def step(index, carry):
@@ -840,29 +899,24 @@
     wide = (levels - 1) * XCOLS
     split = (n_gy.bit_length() - 1) * XCOLS
     matrices, plane, table, perms, interp, stiff, weights = constant_tables()
-    geom = jnp.concatenate(
-        [geometry.reshape(3 * EX, LANES), jnp.ones((8 - 3 * EX, LANES), jnp.float32)], axis=0
-    )
-    force = (disc_mask.astype(jnp.float32) * thrust).reshape(EX, LANES)
-    live = (jnp.arange(XCOLS)[None, :] < col_count).astype(jnp.float32)
-    live = jnp.concatenate(
-        [
-            live[0:1],
-            jnp.zeros((1, LANES - XCOLS), jnp.float32),
-            live[1:].reshape(1, wide),
-        ],
-        axis=1,
-    )
     field = (EX, NODES, 64, LANES)
     f32 = jnp.float32
     out = pl.pallas_call(
         functools.partial(kernel, n_gx, n_gy, levels, interp, stiff, weights),
         out_shape=jax.ShapeDtypeStruct((512, 256), f32),
-        in_specs=[pl.BlockSpec(memory_space=pltpu.VMEM)] * 4
-        + [pl.BlockSpec(memory_space=pl.ANY)] * 2
-        + [pl.BlockSpec(memory_space=pltpu.VMEM)] * 3,
+        in_specs=[pl.BlockSpec(memory_space=pl.ANY)] * 10,
         out_specs=pl.BlockSpec(memory_space=pltpu.VMEM),
         scratch_shapes=[
+            pltpu.VMEM((NODES * NODES * EX * EY, EZ * NODES), f32),
+            pltpu.VMEM(geometry.shape, f32),
+            pltpu.VMEM(disc_mask.shape, jnp.int32),
+            pltpu.VMEM(thrust.shape, f32),
+            pltpu.VMEM(col_count.shape, jnp.int32),
+            pltpu.VMEM(plane.shape, jnp.bfloat16),
+            pltpu.VMEM(table.shape, f32),
+            pltpu.VMEM(perms.shape, jnp.bfloat16),
+            pltpu.VMEM((8, LANES), f32),
+            pltpu.VMEM((1, LANES + wide), f32),
             pltpu.VMEM(field, f32),
             pltpu.VMEM(field, f32),
             pltpu.VMEM(field, f32),
@@ -878,10 +932,10 @@
             pltpu.VMEM(matrices.shape, jnp.bfloat16),
             pltpu.VMEM((2, 2, 2, 64, LANES), f32),
             pltpu.VMEM((2, 2, 8, 8, LANES), f32),
-            pltpu.VMEM((2, 4, 3, 8, LANES), f32),
+            pltpu.VMEM((2, 4, 8, LANES), f32),
             pltpu.VMEM((2, 2, 2, 64, LANES), f32),
             pltpu.VMEM((2, 2, 2, 8, 8, LANES), f32),
-            pltpu.VMEM((2, 4, 3, 8, LANES), f32),
+            pltpu.VMEM((2, 4, 8, LANES), f32),
             pltpu.VMEM((8, 8, LANES), f32),
             pltpu.VMEM((1, wide), f32),
             pltpu.VMEM((CYCLES, n_gy - 1, 1, wide), f32),
@@ -895,16 +949,17 @@
             pltpu.SemaphoreType.DMA((CYCLES, n_gy - 1)),
             pltpu.SemaphoreType.DMA((n_gx - 1,)),
             pltpu.SemaphoreType.DMA((CYCLES, n_gx - 1)),
-            pltpu.SemaphoreType.DMA((2,)),
+            pltpu.SemaphoreType.DMA((10,)),
         ],
         compiler_params=pltpu.CompilerParams(
-            collective_id=0, has_side_effects=True, vmem_limit_bytes=48 * 1024 * 1024
+            collective_id=0, has_side_effects=True, vmem_limit_bytes=56 * 1024 * 1024
         ),
     )(
         source.reshape(NODES * NODES * EX * EY, EZ * NODES),
-        geom,
-        force,
-        live,
+        geometry,
+        disc_mask,
+        thrust,
+        col_count,
         xxt_factor.reshape(levels * XCOLS, xxt_factor.shape[2]),
         jnp.asarray(matrices),
         jnp.asarray(plane),

time: 129 us -> 116 us (0.90)
  Pallas kernels: 118 us -> 111 us
  local copies, waits for them, and re-layouts: 9.07 us -> 5.32 us
  other arithmetic: 1.44 us -> 0 us
    pallas_call x1, Pallas kernels: 118 us -> 111 us  [per_device(): pl.pallas_call(functools.partial(kernel, n_gx, n_gy, levels, interp, stif...]
    unnamed x10 -> x1, local copies, waits for them, and re-layouts: 5.87 us -> 1.33 us
where the time goes in v2:
time: 116 us
  Pallas kernels  111 us (96%)
  local copies, waits for them, and re-layouts  5.32 us (5%)
    pallas_call x1, Pallas kernels, per_device(): pl.pallas_call(functools.partial(kernel, n_gx, n_gy, levels, interp, stif...  111 us

profile of v2, /device:TPU:1, one launch (start us, length us, event | category | flops | bytes accessed | tf_op | source)
XLA Modules:
  0.0 116.2 jit_solution(17086568937438869086)
XLA Ops:
  0.0 1.3 %copy.11.count_hbm = s32[9,1]{1,0:T(8,128)} copy(s32[9,1]{0,1:T(1,128)} %param.15) | data formatting | bytes 72 | tf_op args[5]
  1.3 2.0 %reshape.9.source_hbm = f32[512,256]{1,0:T(8,128)} reshape(f32[8,8,2,4,256]{4,3,2,1,0:T(4,128)} %param.10) | data formatting | bytes 1048576 | tf_op jit(solution)/shard_map/reshape | solution.py:958
  3.3 110.9 %shard_map.100 = f32[512,256]{1,0:T(8,128)} custom-call(f32[512,256]{1,0:T(8,128)} %reshape.9.source_hbm, f32[3,2,4,32]{3,2,1,0:T(4,128)} %lengths_hbm.1, s32[2,4,32]{2,1,0:T(4,128)} %disc_hbm.1, f32[2,4,32]{2,1,0:T(4,128)} %thrust_hbm.1, s32[9,1]{1,0:T(8,128)} %copy.11.count_hbm, f32[288,2048]{1,0:T(8,128)} %bitcast.1, ...), custom_call_target="tpu_custom_call" | custom-call | tf_op jit(solution)/shard_map/pallas_call | solution.py:904
  114.3 2.0 %reshape.11 = f32[8,8,2,4,256]{4,3,2,1,0:T(4,128)} reshape(f32[512,256]{1,0:T(8,128)} %shard_map.100) | data formatting | bytes 1048576 | tf_op jit(solution)/shard_map/reshape | solution.py:969

commit v3 on v2

--- a/solution.py
+++ b/solution.py
@@ -122,6 +122,10 @@
     rows += [values[:, None] * full, weights[:, None] * full, free / z_shared, free * full]
     rows += [interp[:, 0:1] * full, interp[:, 1:2] * full]
     rows += [stiffness[:, c : c + 1] * full for c in range(NODES)]
+    low_side = np.arange(LANES)[None, :] < LANES // 2
+    rows += [
+        np.where(low_side, stiffness[b, 0], stiffness[b, NODES - 1]) * full for b in range(NODES)
+    ]
     table = np.stack(rows).astype(np.float32)
     perm = np.zeros((2 * LANES, 2 * LANES), np.float32)
     for t in range(2):
@@ -195,7 +199,7 @@
     live_ref,
     u_ref,
     r_ref,
-    d_ref,
+    w_ref,
     x_ref,
     weight_ref,
     winv_ref,
@@ -203,6 +207,8 @@
     inv_ref,
     face_lam,
     face_normal,
+    own_lam,
+    own_normal,
     line_tab,
     x_factor_ref,
     mat_ref,
@@ -322,12 +328,12 @@
 
     for half in range(2):
         at = slice(half * LANES, (half + 1) * LANES)
-        d_ref[half] = source_ref[:, at].reshape(8, 64, LANES)
+        w_ref[half] = source_ref[:, at].reshape(8, 64, LANES)
     by_node = exact_rows(
         jnp.concatenate(
             [
                 jnp.concatenate(
-                    [d_ref[half, a, pl.ds(k, 8, stride=8)] for half in range(2)], axis=1
+                    [w_ref[half, a, pl.ds(k, 8, stride=8)] for half in range(2)], axis=1
                 )
                 for k in range(EX * EY)
                 for a in range(NODES)
@@ -383,22 +389,22 @@
         copy.start()
         geom_copies.append(copy)
 
-    def own_pairs():
-        shared = u_ref[0, 7] + u_ref[1, 0]
-        u_ref[0, 7] = shared
-        u_ref[1, 0] = shared
-        low = u_ref[:, :, 0:8]
-        high = u_ref[:, :, 56:64]
-        u_ref[:, :, 0:8] = low + jnp.where(lane >= EZ, roll(high, EZ), 0.0)
-        u_ref[:, :, 56:64] = high + jnp.where(lane < LANES - EZ, roll(low, -EZ), 0.0)
+    def own_pairs(ref):
+        shared = ref[0, 7] + ref[1, 0]
+        ref[0, 7] = shared
+        ref[1, 0] = shared
+        low = ref[:, :, 0:8]
+        high = ref[:, :, 56:64]
+        ref[:, :, 0:8] = low + jnp.where(lane >= EZ, roll(high, EZ), 0.0)
+        ref[:, :, 56:64] = high + jnp.where(lane < LANES - EZ, roll(low, -EZ), 0.0)
         for ex in range(EX):
             for a in range(NODES):
-                low = u_ref[ex, a, pl.ds(0, 8, stride=8)]
-                high = u_ref[ex, a, pl.ds(7, 8, stride=8)]
-                u_ref[ex, a, pl.ds(0, 8, stride=8)] = low + jnp.where(
+                low = ref[ex, a, pl.ds(0, 8, stride=8)]
+                high = ref[ex, a, pl.ds(7, 8, stride=8)]
+                ref[ex, a, pl.ds(0, 8, stride=8)] = low + jnp.where(
                     z2 > 0, roll(high, 1), 0.0
                 )
-                u_ref[ex, a, pl.ds(7, 8, stride=8)] = high + jnp.where(
+                ref[ex, a, pl.ds(7, 8, stride=8)] = high + jnp.where(
                     z2 < EZ - 1, roll(low, -1), 0.0
                 )
 
@@ -425,7 +431,7 @@
             total = term if total is None else total + term
         return total
 
-    def exchange_faces(slot, planes):
+    def send_faces(slot, planes):
         send_x[slot, 0, 0] = u_ref[0, 0]
         send_x[slot, 1, 0] = u_ref[1, 7]
         send_y[slot, 0] = y_faces()
@@ -488,11 +494,14 @@
             )
             copy.start()
             copies.append(copy)
+        return copies
+
+    def receive_faces(slot, copies):
         for copy in copies:
             copy.wait()
         u_ref[1, 7] += recv_x[slot, FROM_RIGHT, 0]
         u_ref[0, 0] += recv_x[slot, FROM_LEFT, 0]
-        add_y(arrived_y(slot, 0))
+        add_y(u_ref, arrived_y(slot, 0))
         for index, (ex, a, first, to_ey) in enumerate(
             ((1, 7, 56, EY - 1), (0, 0, 0, 0), (1, 7, 0, 0), (0, 0, 56, EY - 1))
         ):
@@ -505,10 +514,10 @@
         from_down = recv_y[slot, FROM_DOWN - 2, plane]
         return roll(jnp.where(lane3 >= 2 * EZ, from_down, from_up), 2 * EZ)
 
-    def add_y(plane):
+    def add_y(ref, plane):
         for ex in range(EX):
-            u_ref[ex, :, 0:8] += jnp.where(lane3 < EZ, roll(plane, -EZ * ex), 0.0)
-            u_ref[ex, :, 56:64] += jnp.where(
+            ref[ex, :, 0:8] += jnp.where(lane3 < EZ, roll(plane, -EZ * ex), 0.0)
+            ref[ex, :, 56:64] += jnp.where(
                 lane3 >= 3 * EZ, roll(plane, EZ * (1 - ex)), 0.0
             )
 
@@ -553,7 +562,31 @@
         normal = jnp.concatenate([sides[0], sides[1], normal_y.reshape(64, LANES)], axis=1)
         weight = weight_ref[0] * (1.0 / w_end)
         weight = jnp.concatenate([weight] * 3, axis=1)
-        spread = small_product(1, face_lam[...] * small_product(0, weight * face))
+        odd_ex = lax.rem(lax.div(lane2, EZ), 2) == 1
+        arrived = y_faces() - send_y[slot, 0]
+        arrived = jnp.concatenate(
+            [
+                jnp.where(odd_ex, arrived[0], 0.0)[None],
+                arrived[1:7],
+                jnp.where(odd_ex, 0.0, arrived[7])[None],
+            ],
+            axis=0,
+        )
+        arrived = jnp.concatenate(
+            [
+                u_ref[0, 0] - send_x[slot, 0, 0],
+                u_ref[1, 7] - send_x[slot, 1, 0],
+                arrived.reshape(64, LANES),
+            ],
+            axis=1,
+        )
+        modes = small_product(
+            0, jnp.concatenate([weight * face, weight * arrived], axis=1)
+        )
+        width = 3 * LANES
+        modes = face_lam[...] * modes[:, :width] + own_lam[...] * modes[:, width:]
+        spread = small_product(1, modes)
+        inward = own_normal[...] * arrived
         result = face_normal[...] * (normal + k_end * face) + w_end * weight * spread
         lines = []
         for side in range(2):
@@ -575,14 +608,25 @@
                 + line_tab[side, 1] * (along_y + k_end * value)
                 + line_tab[side, 2] * along_z
             )
-        return result, lines
-
-    def add_outer(result, lines):
+        return result, lines, inward
+
+    def add_outer(result, lines, inward):
+        inward_y = inward[:, 2 * LANES :].reshape(8, 8, LANES)
+        for ex in range(EX):
+            inward_x = inward[:, ex * LANES : (ex + 1) * LANES]
+            along = jnp.where(
+                lane3 < EZ,
+                roll(inward_y, -EZ * ex),
+                jnp.where(lane3 >= 3 * EZ, roll(inward_y, EZ * (1 - ex)), 0.0),
+            )
+            for a in range(NODES):
+                terms = (along[a][None] * tab_ref[46:54]).reshape(64, LANES)
+                w_ref[ex, a] += terms + inward_x * float(stiff[a, 7 * ex])
         for side, (ex, a) in enumerate(((0, 0), (1, 7))):
-            u_ref[ex, a] += result[:, side * LANES : (side + 1) * LANES]
-            u_ref[ex, a, 0:8] += in_slot(lines[side], 0)
-            u_ref[ex, a, 56:64] += in_slot(lines[side], 3)
-        add_y(result[:, 2 * LANES :].reshape(8, 8, LANES))
+            w_ref[ex, a] += result[:, side * LANES : (side + 1) * LANES]
+            w_ref[ex, a, 0:8] += in_slot(lines[side], 0)
+            w_ref[ex, a, 56:64] += in_slot(lines[side], 3)
+        add_y(w_ref, result[:, 2 * LANES :].reshape(8, 8, LANES))
 
     def small_product(which, value):
         high = value.astype(jnp.bfloat16)
@@ -631,12 +675,12 @@
         weight = weight_ref[...]
         out = element_op([u_ref[ex] * weight for ex in range(EX)], lam_ref)
         for ex in range(EX):
-            u_ref[ex] = out[ex] * weight
+            w_ref[ex] = out[ex] * weight
 
     def smoother(keep, take):
         out = element_op([r_ref[ex] for ex in range(EX)], inv_ref)
         for ex in range(EX):
-            u_ref[ex] = (take * out[ex] + keep * d_ref[ex]) * winv_ref[...]
+            u_ref[ex] = (take * out[ex] + keep * u_ref[ex]) * winv_ref[...]
 
     wide = (levels - 1) * XCOLS
     gy_bits = n_gy.bit_length() - 1
@@ -771,10 +815,9 @@
     rho_old = 1.0 / ratio
     rho_new = 1.0 / (2.0 * ratio - rho_old)
 
-    own_pairs()
-    exchange_faces(1, 1)
+    own_pairs(u_ref)
+    receive_faces(1, send_faces(1, 1))
     r_ref[...] = u_ref[...]
-    d_ref[...] = jnp.zeros_like(d_ref)
     x_ref[...] = jnp.zeros_like(x_ref)
 
     for copy in geom_copies:
@@ -805,6 +848,16 @@
         normal, along = (ay, ax) if part == 2 else (ax, ay)
         face_lam[:, at] = ((lam_j * along[None]) + (lam_k * az)[None]).reshape(64, LANES)
         face_normal[:, at] = (w_node * w_c[None] * normal[None]).reshape(64, LANES)
+    own = []
+    for dim in range(3):
+        low, high = (geom_ref[2 * dim + ex : 2 * dim + ex + 1] for ex in range(EX))
+        own.append([low, high, slots([low, roll(high, EZ), roll(low, -EZ), high])])
+    for part in range(3):
+        ax, ay, az = metrics(*[own[dim][part] for dim in range(3)])
+        at = slice(part * LANES, (part + 1) * LANES)
+        normal, along = (ay, ax) if part == 2 else (ax, ay)
+        own_lam[:, at] = ((lam_j * along[None]) + (lam_k * az)[None]).reshape(64, LANES)
+        own_normal[:, at] = (w_node * w_c[None] * normal[None]).reshape(64, LANES)
     for side, (low, high, ex) in enumerate(
         ((FROM_LEFT_DOWN, FROM_LEFT_UP, 1), (FROM_RIGHT_DOWN, FROM_RIGHT_UP, 0))
     ):
@@ -841,20 +894,23 @@
             take = jnp.where(second, 2.0 * rho_new / radius, 1.0 / center)
             smoother(keep, take)
 
-        own_pairs()
-        exchange_faces(slot, 2)
-        for ex in range(EX):
-            d_ref[ex] = u_ref[ex]
-            x_ref[ex] += u_ref[ex]
+        own_pairs(u_ref)
+        copies = send_faces(slot, 2)
 
         @pl.when(index < SMOOTH * CYCLES - 1)
         def _():
-            result, lines = outer_terms(slot)
             stiffness()
-            add_outer(result, lines)
-            own_pairs()
+
+        receive_faces(slot, copies)
+        for ex in range(EX):
+            x_ref[ex] += u_ref[ex]
+
+        @pl.when(index < SMOOTH * CYCLES - 1)
+        def _():
+            add_outer(*outer_terms(slot))
+            own_pairs(w_ref)
             for ex in range(EX):
-                r_ref[ex] -= free_scaled(u_ref[ex])
+                r_ref[ex] -= free_scaled(w_ref[ex])
 
         return carry
 
@@ -886,10 +942,10 @@
         for k in range(EX * EY):
             for a in range(NODES):
                 first = k * 64 + a * 8
-                d_ref[half, a, pl.ds(k, 8, stride=8)] = result[first : first + 8, at]
+                w_ref[half, a, pl.ds(k, 8, stride=8)] = result[first : first + 8, at]
     for half in range(2):
         at = slice(half * LANES, (half + 1) * LANES)
-        out_ref[:, at] = d_ref[half].reshape(512, LANES)
+        out_ref[:, at] = w_ref[half].reshape(512, LANES)
 
 
 def per_device(source, geometry, disc_mask, thrust, xxt_factor, col_count):
@@ -925,6 +981,8 @@
             pltpu.VMEM(field[1:], f32),
             pltpu.VMEM(field, f32),
             pltpu.VMEM(field, f32),
+            pltpu.VMEM((64, 3 * LANES), f32),
+            pltpu.VMEM((64, 3 * LANES), f32),
             pltpu.VMEM((64, 3 * LANES), f32),
             pltpu.VMEM((64, 3 * LANES), f32),
             pltpu.VMEM((2, 3, 8, LANES), f32),

time: 116 us -> 112 us (0.966)
  Pallas kernels: 111 us -> 107 us
    pallas_call x1, Pallas kernels: 111 us -> 107 us  [per_device(): pl.pallas_call(functools.partial(kernel, n_gx, n_gy, levels, interp, stif...]
where the time goes in v3:
time: 112 us
  Pallas kernels  107 us (96%)
  local copies, waits for them, and re-layouts  5.32 us (5%)
    pallas_call x1, Pallas kernels, per_device(): pl.pallas_call(functools.partial(kernel, n_gx, n_gy, levels, interp, stif...  107 us

profile of v3, /device:TPU:1, one launch (start us, length us, event | category | flops | bytes accessed | tf_op | source)
XLA Modules:
  0.0 112.1 jit_solution(12050706960003893633)
XLA Ops:
  0.0 1.3 %copy.11.count_hbm = s32[9,1]{1,0:T(8,128)} copy(s32[9,1]{0,1:T(1,128)} %param.15) | data formatting | bytes 72 | tf_op args[5]
  1.3 2.0 %reshape.9.source_hbm = f32[512,256]{1,0:T(8,128)} reshape(f32[8,8,2,4,256]{4,3,2,1,0:T(4,128)} %param.10) | data formatting | bytes 1048576 | tf_op jit(solution)/shard_map/reshape | solution.py:1016
  3.3 106.8 %shard_map.100 = f32[512,256]{1,0:T(8,128)} custom-call(f32[512,256]{1,0:T(8,128)} %reshape.9.source_hbm, f32[3,2,4,32]{3,2,1,0:T(4,128)} %lengths_hbm.1, s32[2,4,32]{2,1,0:T(4,128)} %disc_hbm.1, f32[2,4,32]{2,1,0:T(4,128)} %thrust_hbm.1, s32[9,1]{1,0:T(8,128)} %copy.11.count_hbm, f32[288,2048]{1,0:T(8,128)} %bitcast.1, ...), custom_call_target="tpu_custom_call" | custom-call | tf_op jit(solution)/shard_map/pallas_call | solution.py:960
  110.1 2.0 %reshape.11 = f32[8,8,2,4,256]{4,3,2,1,0:T(4,128)} reshape(f32[512,256]{1,0:T(8,128)} %shard_map.100) | data formatting | bytes 1048576 | tf_op jit(solution)/shard_map/reshape | solution.py:1027

commit v4 on v3

--- a/solution.py
+++ b/solution.py
@@ -306,7 +306,7 @@
         chosen = [0] * 4 if first == 0 else range(first - 3, first + 1)
         count = None
         for place, level in enumerate(chosen):
-            one = jnp.broadcast_to(count_ref[level : level + 1], (1, LANES))
+            one = jnp.broadcast_to(count_ref[:, level : level + 1], (1, LANES))
             count = one if count is None else jnp.where(lane2 >= XCOLS * place, one, count)
         at = slice(first // 4 * LANES, (first // 4 + 1) * LANES)
         live_ref[:, at] = (column < count).astype(jnp.float32)
@@ -321,14 +321,13 @@
     w_end = float(weights[0])
     k_end = float(stiff[0, 0])
     weight_ref[...] = (w_node[:, None] * w_node[None] * w_c[None, None]).reshape(8, 64, LANES)
-    winv_ref[...] = (edge[:, None] * edge[None] * zmask[None, None]).reshape(8, 64, LANES)
 
     def metrics(hx, hy, hz):
         return hy * hz / (2.0 * hx), hx * hz / (2.0 * hy), hx * hy / (2.0 * hz)
 
     for half in range(2):
         at = slice(half * LANES, (half + 1) * LANES)
-        w_ref[half] = source_ref[:, at].reshape(8, 64, LANES)
+        w_ref[half] = source_ref[:, :, at].reshape(8, 64, LANES)
     by_node = exact_rows(
         jnp.concatenate(
             [
@@ -357,14 +356,6 @@
         hx = geom_ref[ex : ex + 1]
         hy = geom_ref[2 + ex : 3 + ex]
         hz = geom_ref[4 + ex : 5 + ex]
-        ax, ay, az = metrics(hx, hy, hz)
-        in_x = lam_i * ax[None]
-        in_y = lam_j * ay[None]
-        in_z = lam_k * az
-        spectrum = (in_x[:, None] + in_y[None] + in_z[None, None]).reshape(8, 64, LANES)
-        shift = shift_ratio * (ax + ay + az)
-        lam_ref[ex] = spectrum
-        inv_ref[ex] = 1.0 / (spectrum + shift[None])
         mass = (hx * hy * hz / 8.0)[None] * weight_ref[...]
         u_ref[ex] = mass * (u_ref[ex] + forces[ex][None])
 
@@ -373,8 +364,6 @@
 
     for ex in range(EX):
         u_ref[ex] = free_scaled(u_ref[ex])
-
-    pl.semaphore_wait(barrier, len(everyone))
 
     geom_copies = []
     for index, target in enumerate(targets):
@@ -386,7 +375,6 @@
             device_id=target,
             device_id_type=MESH,
         )
-        copy.start()
         geom_copies.append(copy)
 
     def own_pairs(ref):
@@ -432,59 +420,10 @@
         return total
 
     def send_faces(slot, planes):
-        send_x[slot, 0, 0] = u_ref[0, 0]
-        send_x[slot, 1, 0] = u_ref[1, 7]
-        send_y[slot, 0] = y_faces()
-        corners = (
-            (u_ref[0, 0, 0:8], 0),
-            (u_ref[1, 7, 56:64], EY - 1),
-            (u_ref[0, 0, 56:64], EY - 1),
-            (u_ref[1, 7, 0:8], 0),
-        )
-        lines = [roll(value, -EZ * ey) for value, ey in corners]
-        if planes > 1:
-            low = weighted([(a, u_ref[0, a]) for a in range(1, NODES)], 0)
-            high = weighted([(a, u_ref[1, a]) for a in range(NODES - 1)], 7)
-            send_x[slot, 0, 1] = low
-            send_x[slot, 1, 1] = high
-            down_normal, up_normal = [], []
-            for ex in range(EX):
-                rows = [u_ref[ex, :, 8 * b : 8 * b + 8] for b in range(NODES)]
-                down_normal.append(weighted([(b, rows[b]) for b in range(1, NODES)], 0))
-                up_normal.append(weighted([(b, rows[b]) for b in range(NODES - 1)], 7))
-            normal = packed_y(down_normal, up_normal)
-            send_y[slot, 1] = normal
-            along_x = (low[0:8], high[56:64], low[56:64], high[0:8])
-            along_y = ((normal[0], 0), (normal[7], 3), (normal[0], 2), (normal[7], 1))
-            lines = [
-                jnp.where(
-                    lane2 < EZ,
-                    lines[i],
-                    jnp.where(
-                        lane2 < 2 * EZ,
-                        roll(along_x[i], EZ * (1 - corners[i][1])),
-                        roll(along_y[i][0], EZ * (2 - along_y[i][1])),
-                    ),
-                )
-                for i in range(4)
-            ]
-        for i in range(4):
-            send_c[slot, i] = lines[i]
-        pairs = (
-            [
-                (send_x.at[slot, i, pl.ds(0, planes)], recv_x.at[slot, i, pl.ds(0, planes)])
-                for i in range(2)
-            ]
-            + [
-                (send_y.at[slot, pl.ds(0, planes)], recv_y.at[slot, i, pl.ds(0, planes)])
-                for i in range(2)
-            ]
-            + [(send_c.at[slot, i], recv_c.at[slot, i]) for i in range(4)]
-        )
-        copies = []
-        for index in (4, 5, 6, 7, 0, 1, 2, 3):
-            source, landing = pairs[index]
-            copy = pltpu.make_async_remote_copy(
+        copies = [None] * 8
+
+        def start(index, source, landing):
+            copies[index] = pltpu.make_async_remote_copy(
                 src_ref=source,
                 dst_ref=landing,
                 send_sem=send_sem.at[slot, index],
@@ -492,8 +431,51 @@
                 device_id=targets[index],
                 device_id_type=MESH,
             )
-            copy.start()
-            copies.append(copy)
+            copies[index].start()
+
+        corners = ((0, 0, 0), (1, 7, 7), (0, 0, 7), (1, 7, 0))
+        if planes > 1:
+            low = weighted([(a, u_ref[0, a]) for a in range(1, NODES)], 0)
+            high = weighted([(a, u_ref[1, a]) for a in range(NODES - 1)], 7)
+        for i, (ex, a, b) in enumerate(corners):
+            ey = 0 if b == 0 else EY - 1
+            line = roll(u_ref[ex, a, 8 * b : 8 * b + 8], -EZ * ey)
+            if planes > 1:
+                along_x = (high if ex else low)[8 * b : 8 * b + 8]
+                others = [other for other in range(NODES) if other != b]
+                along_y = weighted(
+                    [(other, u_ref[ex, a, 8 * other : 8 * other + 8]) for other in others], b
+                )
+                line = jnp.where(
+                    lane2 < EZ,
+                    line,
+                    jnp.where(
+                        lane2 < 2 * EZ,
+                        roll(along_x, EZ * (1 - ey)),
+                        roll(along_y, EZ * (2 - ey)),
+                    ),
+                )
+            send_c[slot, i] = line
+        for i in range(4):
+            start(4 + i, send_c.at[slot, i], recv_c.at[slot, i])
+        send_x[slot, 0, 0] = u_ref[0, 0]
+        send_x[slot, 1, 0] = u_ref[1, 7]
+        if planes > 1:
+            send_x[slot, 0, 1] = low
+            send_x[slot, 1, 1] = high
+        both = pl.ds(0, planes)
+        for i in range(2):
+            start(i, send_x.at[slot, i, both], recv_x.at[slot, i, both])
+        send_y[slot, 0] = y_faces()
+        if planes > 1:
+            down_normal, up_normal = [], []
+            for ex in range(EX):
+                rows = [u_ref[ex, :, 8 * b : 8 * b + 8] for b in range(NODES)]
+                down_normal.append(weighted([(b, rows[b]) for b in range(1, NODES)], 0))
+                up_normal.append(weighted([(b, rows[b]) for b in range(NODES - 1)], 7))
+            send_y[slot, 1] = packed_y(down_normal, up_normal)
+        for i in range(2):
+            start(2 + i, send_y.at[slot, both], recv_y.at[slot, i, both])
         return copies
 
     def receive_faces(slot, copies):
@@ -816,38 +798,26 @@
     rho_new = 1.0 / (2.0 * ratio - rho_old)
 
     own_pairs(u_ref)
-    receive_faces(1, send_faces(1, 1))
-    r_ref[...] = u_ref[...]
+    pl.semaphore_wait(barrier, len(everyone))
+    copies = send_faces(1, 1)
+    for copy in geom_copies:
+        copy.start()
+    winv_ref[...] = (edge[:, None] * edge[None] * zmask[None, None]).reshape(8, 64, LANES)
+    for ex in range(EX):
+        ax, ay, az = metrics(*[geom_ref[2 * dim + ex : 2 * dim + ex + 1] for dim in range(3)])
+        in_x = lam_i * ax[None]
+        in_y = lam_j * ay[None]
+        in_z = lam_k * az
+        spectrum = (in_x[:, None] + in_y[None] + in_z[None, None]).reshape(8, 64, LANES)
+        shift = shift_ratio * (ax + ay + az)
+        lam_ref[ex] = spectrum
+        inv_ref[ex] = 1.0 / (spectrum + shift[None])
     x_ref[...] = jnp.zeros_like(x_ref)
-
-    for copy in geom_copies:
-        copy.wait()
     slots = lambda values: jnp.where(
         lane2 < EZ,
         values[0],
         jnp.where(lane2 < 2 * EZ, values[1], jnp.where(lane2 < 3 * EZ, values[2], values[3])),
     )
-
-    def ghost(source, dim, ex):
-        return recv_g[source, 2 * dim + ex : 2 * dim + ex + 1]
-
-    outer = []
-    for dim in range(3):
-        y_side = slots(
-            [
-                roll(ghost(FROM_DOWN, dim, 0), EZ),
-                roll(ghost(FROM_DOWN, dim, 1), 2 * EZ),
-                roll(ghost(FROM_UP, dim, 0), 2 * EZ),
-                roll(ghost(FROM_UP, dim, 1), 3 * EZ),
-            ]
-        )
-        outer.append([ghost(FROM_LEFT, dim, 1), ghost(FROM_RIGHT, dim, 0), y_side])
-    for part in range(3):
-        ax, ay, az = metrics(*[outer[dim][part] for dim in range(3)])
-        at = slice(part * LANES, (part + 1) * LANES)
-        normal, along = (ay, ax) if part == 2 else (ax, ay)
-        face_lam[:, at] = ((lam_j * along[None]) + (lam_k * az)[None]).reshape(64, LANES)
-        face_normal[:, at] = (w_node * w_c[None] * normal[None]).reshape(64, LANES)
     own = []
     for dim in range(3):
         low, high = (geom_ref[2 * dim + ex : 2 * dim + ex + 1] for ex in range(EX))
@@ -858,6 +828,31 @@
         normal, along = (ay, ax) if part == 2 else (ax, ay)
         own_lam[:, at] = ((lam_j * along[None]) + (lam_k * az)[None]).reshape(64, LANES)
         own_normal[:, at] = (w_node * w_c[None] * normal[None]).reshape(64, LANES)
+    receive_faces(1, copies)
+    r_ref[...] = u_ref[...]
+    for copy in geom_copies:
+        copy.wait()
+
+    def ghost(source, dim, ex):
+        return recv_g[source, 2 * dim + ex : 2 * dim + ex + 1]
+
+    outer = []
+    for dim in range(3):
+        y_side = slots(
+            [
+                roll(ghost(FROM_DOWN, dim, 0), EZ),
+                roll(ghost(FROM_DOWN, dim, 1), 2 * EZ),
+                roll(ghost(FROM_UP, dim, 0), 2 * EZ),
+                roll(ghost(FROM_UP, dim, 1), 3 * EZ),
+            ]
+        )
+        outer.append([ghost(FROM_LEFT, dim, 1), ghost(FROM_RIGHT, dim, 0), y_side])
+    for part in range(3):
+        ax, ay, az = metrics(*[outer[dim][part] for dim in range(3)])
+        at = slice(part * LANES, (part + 1) * LANES)
+        normal, along = (ay, ax) if part == 2 else (ax, ay)
+        face_lam[:, at] = ((lam_j * along[None]) + (lam_k * az)[None]).reshape(64, LANES)
+        face_normal[:, at] = (w_node * w_c[None] * normal[None]).reshape(64, LANES)
     for side, (low, high, ex) in enumerate(
         ((FROM_LEFT_DOWN, FROM_LEFT_UP, 1), (FROM_RIGHT_DOWN, FROM_RIGHT_UP, 0))
     ):
@@ -945,7 +940,7 @@
                 w_ref[half, a, pl.ds(k, 8, stride=8)] = result[first : first + 8, at]
     for half in range(2):
         at = slice(half * LANES, (half + 1) * LANES)
-        out_ref[:, at] = w_ref[half].reshape(512, LANES)
+        out_ref[:, :, at] = w_ref[half].reshape(128, EY, LANES)
 
 
 def per_device(source, geometry, disc_mask, thrust, xxt_factor, col_count):
@@ -959,15 +954,15 @@
     f32 = jnp.float32
     out = pl.pallas_call(
         functools.partial(kernel, n_gx, n_gy, levels, interp, stiff, weights),
-        out_shape=jax.ShapeDtypeStruct((512, 256), f32),
+        out_shape=jax.ShapeDtypeStruct((NODES * NODES * EX, EY, EZ * NODES), f32),
         in_specs=[pl.BlockSpec(memory_space=pl.ANY)] * 10,
         out_specs=pl.BlockSpec(memory_space=pltpu.VMEM),
         scratch_shapes=[
-            pltpu.VMEM((NODES * NODES * EX * EY, EZ * NODES), f32),
+            pltpu.VMEM((NODES * NODES * EX, EY, EZ * NODES), f32),
             pltpu.VMEM(geometry.shape, f32),
             pltpu.VMEM(disc_mask.shape, jnp.int32),
             pltpu.VMEM(thrust.shape, f32),
-            pltpu.VMEM(col_count.shape, jnp.int32),
+            pltpu.VMEM((1, levels), jnp.int32),
             pltpu.VMEM(plane.shape, jnp.bfloat16),
             pltpu.VMEM(table.shape, f32),
             pltpu.VMEM(perms.shape, jnp.bfloat16),
@@ -1013,11 +1008,11 @@
             collective_id=0, has_side_effects=True, vmem_limit_bytes=56 * 1024 * 1024
         ),
     )(
-        source.reshape(NODES * NODES * EX * EY, EZ * NODES),
+        source.reshape(NODES * NODES * EX, EY, EZ * NODES),
         geometry,
         disc_mask,
         thrust,
-        col_count,
+        col_count.T,
         xxt_factor.reshape(levels * XCOLS, xxt_factor.shape[2]),
         jnp.asarray(matrices),
         jnp.asarray(plane),

time: 112 us -> 109 us (0.973)
  local copies, waits for them, and re-layouts: 5.32 us -> 1.87 us
    reshape x2 -> x0, local copies, waits for them, and re-layouts: 3.99 us -> none  [the longest x1 2.01 us: per_device(): source.reshape(NODES * NODES * EX * EY, EZ * NODES)]
where the time goes in v4:
time: 109 us; the launch traced here: 108 us
  Pallas kernels  107 us (98%)
  local copies, waits for them, and re-layouts  1.87 us (2%)
    pallas_call x1, Pallas kernels, per_device(): pl.pallas_call(functools.partial(kernel, n_gx, n_gy, levels, interp, stif...  107 us

profile of v4, /device:TPU:1, one launch (start us, length us, event | category | flops | bytes accessed | tf_op | source)
XLA Modules:
  0.0 108.4 jit_solution(8298400903620585463)
XLA Ops:
  0.0 106.5 %shard_map.100 = f32[128,4,256]{2,1,0:T(4,128)} custom-call(f32[128,4,256]{2,1,0:T(4,128)} %bitcast.6, f32[3,2,4,32]{3,2,1,0:T(4,128)} %lengths_hbm.1, s32[2,4,32]{2,1,0:T(4,128)} %disc_hbm.1, f32[2,4,32]{2,1,0:T(4,128)} %thrust_hbm.1, s32[1,9]{1,0:T(1,128)} %bitcast.7, f32[288,2048]{1,0:T(8,128)} %bitcast.4, bf16[4,256,768]{2,1,0:T(8,128)(2,1)} %constant.8.clone.mat_hbm, ...), custom_call_target="tpu_custom_call" | custom-call | tf_op jit(solution)/shard_map/pallas_call | solution.py:955
  106.5 1.9 %copy.12 = f32[8,8,2,4,256]{4,3,2,1,0:T(4,128)} copy(f32[8,8,2,4,256]{4,3,2,1,0:T(4,128)} %bitcast.5) | data formatting | bytes 1048576

commit v5 on v4

--- a/solution.py
+++ b/solution.py
@@ -681,8 +681,7 @@
             )
             copy.start()
             copies.append(copy)
-        for copy in copies:
-            copy.wait()
+        return copies
 
     def level_sum(own, recv_ref, cycle, count, first_level_lane):
         which = lax.broadcasted_iota(jnp.int32, own.shape, 1)
@@ -739,33 +738,41 @@
         upper = jnp.concatenate(
             [row_of(pieces[i : i + 4]) for i in range(1, levels, 4)], axis=1
         )[:, :wide]
+        back = [None] * 8
+
+        def spread(first_level, row):
+            part = jnp.broadcast_to(row, (LANES, LANES)).T
+            for q in range(8):
+                for k in range(row_levels[first_level]):
+                    level = first_level + k
+                    col = part[k * XCOLS : (k + 1) * XCOLS]
+                    block = x_factor_ref[
+                        level * XCOLS : (level + 1) * XCOLS, q * 256 : (q + 1) * 256
+                    ]
+                    term = block * jnp.concatenate([col, col], axis=1)
+                    back[q] = term if back[q] is None else back[q] + term
+
+        def tiles(row):
+            return [row[:, i : i + LANES] for i in range(0, row.shape[1], LANES)]
+
+        row_levels = {0: 1}
+        row_levels.update({level: 4 for level in range(1, levels, 4)})
         send_one[...] = upper
-        exchange(cycle, send_one, recv_one, one_targets, one_send_sem, one_recv_sem)
+        copies = exchange(cycle, send_one, recv_one, one_targets, one_send_sem, one_recv_sem)
+        spread(0, own * live_ref[:, 0:LANES])
+        for copy in copies:
+            copy.wait()
         upper = level_sum(upper, recv_one, cycle, n_gy, 0)
         send_two[...] = upper[:, split:]
-        exchange(cycle, send_two, recv_two, two_targets, two_send_sem, two_recv_sem)
+        copies = exchange(cycle, send_two, recv_two, two_targets, two_send_sem, two_recv_sem)
+        for i, row in enumerate(tiles(upper[:, :split] * live_ref[:, LANES : LANES + split])):
+            spread(1 + 4 * i, row)
+        for copy in copies:
+            copy.wait()
         top = level_sum(upper[:, split:], recv_two, cycle, n_gx, 0)
-        upper = jnp.concatenate([upper[:, :split], top], axis=1)
-        own = own * live_ref[:, 0:LANES]
-        upper = upper * live_ref[:, LANES : LANES + wide]
-        tail = (-wide) % LANES
-        if tail:
-            upper = jnp.concatenate([upper, jnp.zeros((1, tail), jnp.float32)], axis=1)
-        cols = [jnp.broadcast_to(own, (LANES, LANES)).T[:XCOLS]]
-        for first in range(0, wide, LANES):
-            part = jnp.broadcast_to(upper[:, first : first + LANES], (LANES, LANES)).T
-            cols += [part[k * XCOLS : (k + 1) * XCOLS] for k in range(LANES // XCOLS)]
-        back = []
-        for q in range(8):
-            acc = None
-            for level in range(levels):
-                block = x_factor_ref[
-                    level * XCOLS : (level + 1) * XCOLS, q * 256 : (q + 1) * 256
-                ]
-                col = cols[level]
-                term = block * jnp.concatenate([col, col], axis=1)
-                acc = term if acc is None else acc + term
-            back.append(jnp.sum(acc, axis=0, keepdims=True))
+        for i, row in enumerate(tiles(top * live_ref[:, LANES + split : LANES + wide])):
+            spread(1 + split // XCOLS + 4 * i, row)
+        back = [jnp.sum(total, axis=0, keepdims=True) for total in back]
         split_t = exact_rows(jnp.concatenate(back, axis=0), perm_ref[1])
         for ex in range(EX):
             by_v = []
@@ -892,24 +899,23 @@
         own_pairs(u_ref)
         copies = send_faces(slot, 2)
 
-        @pl.when(index < SMOOTH * CYCLES - 1)
-        def _():
-            stiffness()
-
+        stiffness()
         receive_faces(slot, copies)
         for ex in range(EX):
             x_ref[ex] += u_ref[ex]
-
-        @pl.when(index < SMOOTH * CYCLES - 1)
-        def _():
-            add_outer(*outer_terms(slot))
-            own_pairs(w_ref)
-            for ex in range(EX):
-                r_ref[ex] -= free_scaled(w_ref[ex])
-
+        add_outer(*outer_terms(slot))
+        own_pairs(w_ref)
+        for ex in range(EX):
+            r_ref[ex] -= free_scaled(w_ref[ex])
         return carry
 
-    lax.fori_loop(0, SMOOTH * CYCLES, step, 0)
+    last = SMOOTH * CYCLES - 1
+    lax.fori_loop(0, last, step, 0)
+    smoother(rho_new * rho_old, 2.0 * rho_new / radius)
+    own_pairs(u_ref)
+    receive_faces(last % 2, send_faces(last % 2, 1))
+    for ex in range(EX):
+        x_ref[ex] += u_ref[ex]
 
     by_node = [
         [

time: 109 us -> 108 us (level)
  no operation moved by 1% of the time
where the time goes in v5:
time: 108 us
  Pallas kernels  106 us (98%)
  local copies, waits for them, and re-layouts  1.87 us (2%)
    pallas_call x1, Pallas kernels, per_device(): pl.pallas_call(functools.partial(kernel, n_gx, n_gy, levels, interp, stif...  106 us

profile of v5, /device:TPU:1, one launch (start us, length us, event | category | flops | bytes accessed | tf_op | source)
XLA Modules:
  0.0 107.8 jit_solution(8838754056486548415)
XLA Ops:
  0.0 105.9 %shard_map.100 = f32[128,4,256]{2,1,0:T(4,128)} custom-call(f32[128,4,256]{2,1,0:T(4,128)} %bitcast.6, f32[3,2,4,32]{3,2,1,0:T(4,128)} %lengths_hbm.1, s32[2,4,32]{2,1,0:T(4,128)} %disc_hbm.1, f32[2,4,32]{2,1,0:T(4,128)} %thrust_hbm.1, s32[1,9]{1,0:T(1,128)} %bitcast.7, f32[288,2048]{1,0:T(8,128)} %bitcast.4, bf16[4,256,768]{2,1,0:T(8,128)(2,1)} %constant.8.clone.mat_hbm, ...), custom_call_target="tpu_custom_call" | custom-call | tf_op jit(solution)/shard_map/pallas_call | solution.py:961
  105.9 1.9 %copy.12 = f32[8,8,2,4,256]{4,3,2,1,0:T(4,128)} copy(f32[8,8,2,4,256]{4,3,2,1,0:T(4,128)} %bitcast.5) | data formatting | bytes 1048576

commit v6 on v5

--- a/solution.py
+++ b/solution.py
@@ -478,18 +478,24 @@
             start(2 + i, send_y.at[slot, both], recv_y.at[slot, i, both])
         return copies
 
-    def receive_faces(slot, copies):
-        for copy in copies:
+    def receive_faces(slot, copies, refs):
+        for copy in copies[2:4]:
             copy.wait()
-        u_ref[1, 7] += recv_x[slot, FROM_RIGHT, 0]
-        u_ref[0, 0] += recv_x[slot, FROM_LEFT, 0]
-        add_y(u_ref, arrived_y(slot, 0))
+        for ref in refs:
+            add_y(ref, arrived_y(slot, 0))
+        for copy in copies[0:2]:
+            copy.wait()
+        for ref in refs:
+            ref[1, 7] += recv_x[slot, FROM_RIGHT, 0]
+            ref[0, 0] += recv_x[slot, FROM_LEFT, 0]
+        for copy in copies[4:8]:
+            copy.wait()
         for index, (ex, a, first, to_ey) in enumerate(
             ((1, 7, 56, EY - 1), (0, 0, 0, 0), (1, 7, 0, 0), (0, 0, 56, EY - 1))
         ):
-            u_ref[ex, a, first : first + 8] += in_slot(
-                roll(recv_c[slot, index], EZ * to_ey), to_ey
-            )
+            line = in_slot(roll(recv_c[slot, index], EZ * to_ey), to_ey)
+            for ref in refs:
+                ref[ex, a, first : first + 8] += line
 
     def arrived_y(slot, plane):
         from_up = recv_y[slot, FROM_UP - 2, plane]
@@ -835,7 +841,7 @@
         normal, along = (ay, ax) if part == 2 else (ax, ay)
         own_lam[:, at] = ((lam_j * along[None]) + (lam_k * az)[None]).reshape(64, LANES)
         own_normal[:, at] = (w_node * w_c[None] * normal[None]).reshape(64, LANES)
-    receive_faces(1, copies)
+    receive_faces(1, copies, (u_ref,))
     r_ref[...] = u_ref[...]
     for copy in geom_copies:
         copy.wait()
@@ -900,9 +906,9 @@
         copies = send_faces(slot, 2)
 
         stiffness()
-        receive_faces(slot, copies)
         for ex in range(EX):
             x_ref[ex] += u_ref[ex]
+        receive_faces(slot, copies, (u_ref, x_ref))
         add_outer(*outer_terms(slot))
         own_pairs(w_ref)
         for ex in range(EX):
@@ -913,9 +919,10 @@
     lax.fori_loop(0, last, step, 0)
     smoother(rho_new * rho_old, 2.0 * rho_new / radius)
     own_pairs(u_ref)
-    receive_faces(last % 2, send_faces(last % 2, 1))
+    copies = send_faces(last % 2, 1)
     for ex in range(EX):
         x_ref[ex] += u_ref[ex]
+    receive_faces(last % 2, copies, (x_ref,))
 
     by_node = [
         [

time: 108 us -> 107 us (level)
  no operation moved by 1% of the time
where the time goes in v6:
time: 107 us
  Pallas kernels  105 us (98%)
  local copies, waits for them, and re-layouts  1.87 us (2%)
    pallas_call x1, Pallas kernels, per_device(): pl.pallas_call(functools.partial(kernel, n_gx, n_gy, levels, interp, stif...  105 us

profile of v6, /device:TPU:1, one launch (start us, length us, event | category | flops | bytes accessed | tf_op | source)
XLA Modules:
  0.0 106.7 jit_solution(4848612828430675137)
XLA Ops:
  0.0 104.8 %shard_map.100 = f32[128,4,256]{2,1,0:T(4,128)} custom-call(f32[128,4,256]{2,1,0:T(4,128)} %bitcast.6, f32[3,2,4,32]{3,2,1,0:T(4,128)} %lengths_hbm.1, s32[2,4,32]{2,1,0:T(4,128)} %disc_hbm.1, f32[2,4,32]{2,1,0:T(4,128)} %thrust_hbm.1, s32[1,9]{1,0:T(1,128)} %bitcast.7, f32[288,2048]{1,0:T(8,128)} %bitcast.4, bf16[4,256,768]{2,1,0:T(8,128)(2,1)} %constant.8.clone.mat_hbm, ...), custom_call_target="tpu_custom_call" | custom-call | tf_op jit(solution)/shard_map/pallas_call | solution.py:968
  104.8 1.9 %copy.12 = f32[8,8,2,4,256]{4,3,2,1,0:T(4,128)} copy(f32[8,8,2,4,256]{4,3,2,1,0:T(4,128)} %bitcast.5) | data formatting | bytes 1048576
